TPU v7x, 128 devices: a whole 4x4x4 slice. The times are simulated.
128 devices in a mesh: edge: 16 (over y, z), node: 8 (over x, core).
Axes of the slice: x: 4, y: 4, z: 4, core: 2. Of those that a mesh axis runs over, the one named last changes fastest.
Arguments:
- residual: float32 [64, 131072], P(None, ('edge', 'node')), may hold values from -6 to 6
- tangent: float32 [3, 64, 131072], P(None, None, ('edge', 'node')), may hold values from -4 to 4
- jacobi: float32 [64, 131072], P(None, ('edge', 'node')), may hold values from 0.2 to 1
- ends: int32 [2, 64, 131072], P(None, None, ('edge', 'node')), may hold values from 0 to 31, as said below
- target: int32 [131072, 1], P(('edge', 'node')), may hold values from 0 to 127; in each aligned block of 1024 rows (0 to 1023, 1024 to 2047, ...) at most 16 rows name the same one
- node_block: int32 [131072], P(('edge', 'node')), may hold values from 0 to 1023
- sigma: float32 [512, 32, 256], P(('edge', 'node')), may hold values from 0.25 to 8
Outputs:
- correction: float32 [64, 131072], P(None, ('edge', 'node'))
Inputs may be any that keep to these rules, and one draw needn't show every extreme that they name: `ends`: the head and tail of an edge differ. `target`: among the 1024 rows of one device no device is named more than 16 times, and one is named exactly 16 times.
All inputs are finite; a program needn't handle non-finite values.
Results may differ from a plain program's by a relative error of at most 0.000086.
Values sent between devices are 32-bit elements; how exact they have to be, the bound alone decides.
No kernel may reach another device: no remote copies, remote signals or barrier semaphores. Data moves between devices by JAX's collectives and lax.ppermute only.
A program may use at most 64 MiB of HBM per device.

v0:
```python
import math

import jax
import jax.numpy as jnp
from jax import lax
from jax.sharding import PartitionSpec as P

BLOCK_EDGES = 64
NODE_BLOCK = 32


mass_scale = (1.0, 1.0, 1.0, 0.5)


def with_halo(cells, sides, width):
    for axis, dim in sides:
        count = lax.axis_size(axis)
        head = lax.slice_in_dim(cells, 0, width, axis=dim)
        tail = lax.slice_in_dim(cells, cells.shape[dim] - width, cells.shape[dim], axis=dim)
        cells = jnp.concatenate(
            [
                lax.ppermute(tail, axis, [(i, (i + 1) % count) for i in range(count)]),
                cells,
                lax.ppermute(head, axis, [((i + 1) % count, i) for i in range(count)]),
            ],
            axis=dim,
        )
    return cells


def chebyshev_terms():
    scale = jnp.array(mass_scale, jnp.float32).reshape(4, 1, 1, 1)
    upper = 12.0 + 8.0 * scale
    lower = upper / 8.0
    centre = (upper + lower) / 2.0
    radius = (upper - lower) / 2.0
    ratio = centre / radius
    first = 1.0 / ratio
    second = 1.0 / (2.0 * ratio - first)
    return (scale, centre, second * first, 2.0 * second / radius)


def stiffness(padded, diag):
    centre = padded[:, 1:-1]
    beside_all = padded[:, :-2] + padded[:, 2:]
    inner = jnp.pad(centre, ((0, 0), (0, 0), (1, 1), (1, 1)))
    beside_all = beside_all + inner[:, :, :-2, 1:-1] + inner[:, :, 2:, 1:-1]
    beside_all = beside_all + inner[:, :, 1:-1, :-2] + inner[:, :, 1:-1, 2:]
    return diag * centre - beside_all


def hot_pair(ends_part):
    node_ids = jnp.arange(NODE_BLOCK, dtype=jnp.int32)[None, :, None]
    head_hot = (ends_part[1][:, None, :] == node_ids).astype(jnp.float32)
    tail_hot = (ends_part[0][:, None, :] == node_ids).astype(jnp.float32)
    return (head_hot, tail_hot)


def group_last(array, group_size):
    leading = array.shape[:-1]
    groups = array.shape[-1] // group_size
    return jnp.moveaxis(array.reshape(leading + (groups, group_size)), -2, 0)


def block_terms(residual, tangent, ends, group_size):
    width = 4 * NODE_BLOCK
    highest = lax.Precision.HIGHEST

    def block_one_group(pieces):
        resid_part, tangent_part, ends_part = pieces
        head_hot, tail_hot = hot_pair(ends_part)
        vector_part = 0.5 * tangent_part * resid_part[None]
        vector_out = jnp.einsum("ceb,enb->bcn", vector_part, head_hot + tail_hot, precision=highest)
        scalar_out = jnp.einsum("eb,enb->bn", resid_part, head_hot - tail_hot, precision=highest)
        return jnp.concatenate([vector_out, scalar_out[:, None]], axis=1).reshape(group_size, width)

    grouped = lax.map(
        block_one_group,
        (
            group_last(residual, group_size),
            group_last(tangent, group_size),
            group_last(ends, group_size),
        ),
    )
    return grouped.reshape(-1, width)


def lift_values(values, tangent, ends, group_size):
    highest = lax.Precision.HIGHEST
    groups = values.shape[0] // group_size
    value_groups = values.reshape(groups, group_size, 4, NODE_BLOCK)

    def lift_one_group(pieces):
        value_part, tangent_part, ends_part = pieces
        head_hot, tail_hot = hot_pair(ends_part)
        vector_sum = jnp.einsum(
            "bcn,enb->ceb", value_part[:, :3], head_hot + tail_hot, precision=highest
        )
        scalar_diff = jnp.einsum(
            "bn,enb->eb", value_part[:, 3], head_hot - tail_hot, precision=highest
        )
        return 0.5 * jnp.sum(tangent_part * vector_sum, axis=0) + scalar_diff

    lifted = lax.map(
        lift_one_group,
        (value_groups, group_last(tangent, group_size), group_last(ends, group_size)),
    )
    return jnp.moveaxis(lifted, 0, 1).reshape(BLOCK_EDGES, -1)


def per_device(residual, tangent, jacobi, ends, target, node_block, sigma):
    devices = lax.axis_size(("edge", "node"))
    blocks_mine = residual.shape[1]
    group_size = math.gcd(blocks_mine, 512)
    capacity = max(2, 2 * blocks_mine // devices)
    slots_all = devices * capacity
    slices, rows_radial, rows_axial = sigma.shape
    nodal_blocks = slices * rows_radial * rows_axial // NODE_BLOCK
    width = 4 * NODE_BLOCK
    target_dev = target[:, 0]
    matches = (target_dev[:, None] == jnp.arange(devices, dtype=jnp.int32)[None, :]).astype(
        jnp.int32
    )
    ranking = jnp.cumsum(matches, axis=0)
    slot_rank = jnp.sum(ranking * matches, axis=1) - 1
    position = target_dev * capacity + slot_rank
    labels = jnp.full((slots_all,), -1, jnp.int32).at[position].set(node_block)
    block_rows = block_terms(residual, tangent, ends, group_size)
    partials = jnp.zeros((slots_all, width), jnp.float32).at[position].set(block_rows)
    got_terms, got_labels = (
        lax.all_to_all(
            partials.reshape(devices, capacity, width),
            ("edge", "node"),
            split_axis=0,
            concat_axis=0,
            tiled=True,
        ),
        lax.all_to_all(
            labels.reshape(devices, capacity),
            ("edge", "node"),
            split_axis=0,
            concat_axis=0,
            tiled=True,
        ),
    )
    got_terms = got_terms.reshape(slots_all, width)
    got_labels = got_labels.reshape(slots_all)
    safe_labels = jnp.where(got_labels < 0, nodal_blocks, got_labels)
    summed = jax.ops.segment_sum(got_terms, safe_labels, num_segments=nodal_blocks + 1)[
        :nodal_blocks
    ]
    source = summed.reshape(slices, rows_radial * rows_axial // NODE_BLOCK, 4, NODE_BLOCK)
    source = source.transpose(2, 0, 1, 3).reshape(4, slices, rows_radial, rows_axial)
    scale, centre, coef_one, coef_two = chebyshev_terms()
    diag = 6.0 + scale * sigma[None]

    def apply(field):
        padded = with_halo(field, ((("edge", "node"), 1),), 1)
        return stiffness(padded, diag)

    step_one = source / centre
    rest = source - apply(step_one)
    step_two = coef_one * step_one + coef_two * rest
    solution = step_one + step_two
    rest = source - apply(solution)
    step_one = rest / centre
    rest = rest - apply(step_one)
    step_two = coef_one * step_one + coef_two * rest
    solution = solution + step_one + step_two
    sol_blocks = solution.reshape(4, slices, rows_radial * rows_axial // NODE_BLOCK, NODE_BLOCK)
    sol_blocks = sol_blocks.transpose(1, 2, 0, 3).reshape(nodal_blocks, width)
    outgoing = sol_blocks[jnp.clip(got_labels, 0, nodal_blocks - 1)]
    returned = lax.all_to_all(
        outgoing.reshape(devices, capacity, width),
        ("edge", "node"),
        split_axis=0,
        concat_axis=0,
        tiled=True,
    )
    mine = returned.reshape(slots_all, width)[position]
    lifted = lift_values(mine, tangent, ends, group_size)
    return jacobi * residual + lifted


def solution(mesh):
    in_specs = (
        P(None, ("edge", "node")),
        P(None, None, ("edge", "node")),
        P(None, ("edge", "node")),
        P(None, None, ("edge", "node")),
        P(("edge", "node"), None),
        P(("edge", "node")),
        P(("edge", "node"), None, None),
    )
    out_specs = P(None, ("edge", "node"))
    return jax.shard_map(
        per_device, mesh=mesh, in_specs=in_specs, out_specs=out_specs, check_vma=False
    )
```

profile of v0, /device:TPU:1, one launch (start us, length us, event | category | flops | bytes accessed | tf_op | source)
XLA Modules:
  0.0 269.8 jit_solution(18098477573437723908)
XLA Ops:
  1.7 4.5 %scatter_custom_fusion = s32[2048]{0:T(1024)S(1)} fusion(s32[1024]{0:T(1024)S(1)} %bitcast.124, s32[1024]{0:T(1024)} %param.17, s32[]{:T(128)} %constant.36.clone.1), kind=kCustom, calls=%fused_computation.110 | custom fusion | bytes 8704 | tf_op jit(solution)/shard_map/scatter | solution.py:127
  6.9 11.5 %all-to-all-start = ((s32[128,1,16]{2,1,0:T(1,128)}), s32[128,1,16]{2,1,0:T(1,128)S(1)}, u32[]{:S(2)}, u32[]{:S(2)}) async-start(s32[128,1,16]{2,1,0:T(1,128)} %bitcast.30), calls=%async_computation | async-start | bytes 131072 | tf_op jit(solution)/shard_map/all_to_all | solution.py:138
  18.4 1.8 copy.42
  22.0 72.9 %while.20 = (s32[]{:T(128)}, f32[2,512,128]{2,1,0:T(8,128)}, f32[2,3,64,512]{2,1,3,0:T(4,128)}, f32[2,64,512]{1,2,0:T(8,128)}, s32[2,2,64,512]{2,3,1,0:T(8,128)S(1)}, /*index=5*/s32[]{:T(128)}, s32[]{:T(128)}, s32[]{}) while((s32[]{:T(128)}, f32[2,512,128]{2,1,0:T(8,128)}, f32[2,3,64,512]{2,1,3,0:T(4,128)}, f32[2,64,512]{1,2,0:T(8,128)}, ...), condition=%wide.region_5.6_spmd, body=%wide.region_4.5_spmd.sunk | while | flops 61014016 | bytes 9306793 | solution.py:77
  23.3 15.5 %fusion.69 = f32[512,3,32]{2,1,0:T(4,128)S(1)} fusion(s32[64,512]{0,1:T(8,128)S(1)} %get-tuple-element.191, s32[64,512]{0,1:T(8,128)S(1)} %get-tuple-element.192, f32[2,3,64,512]{2,1,3,0:T(4,128)} %get-tuple-element.219, s32[]{:T(128)} %get-tuple-element.209, f32[64,512]{0,1:T(8,128)S(1)} %get-tuple-element.193), kind=kOutput, calls=%fused_computation.7.clone.1 | convolution fusion | flops 43089920 | bytes 1638912 | tf_op jit(solution)/shard_map/while/body/eval_jaxpr/ceb,enb->bcn/dot_general | solution.py:73
  39.0 14.0 %fusion.68 = f32[512,1,32]{2,1,0:T(1,128)S(1)} fusion(f32[64,512,1]{0,2,1:T(1,128)S(1)} %bitcast.113, s32[64,512]{0,1:T(8,128)S(1)} %get-tuple-element.191, s32[64,512]{0,1:T(8,128)S(1)} %get-tuple-element.192), kind=kOutput, calls=%fused_computation.8.clone.1 | convolution fusion | flops 17825792 | bytes 458752 | tf_op jit(solution)/shard_map/while/body/eval_jaxpr/eb,enb->bn/dot_general | solution.py:74
  55.2 15.5 %fusion.69 = f32[512,3,32]{2,1,0:T(4,128)S(1)} fusion(s32[64,512]{0,1:T(8,128)S(1)} %get-tuple-element.191, s32[64,512]{0,1:T(8,128)S(1)} %get-tuple-element.192, f32[2,3,64,512]{2,1,3,0:T(4,128)} %get-tuple-element.219, s32[]{:T(128)} %get-tuple-element.209, f32[64,512]{0,1:T(8,128)S(1)} %get-tuple-element.193), kind=kOutput, calls=%fused_computation.7.clone.1 | convolution fusion | flops 43089920 | bytes 1638912 | tf_op jit(solution)/shard_map/while/body/eval_jaxpr/ceb,enb->bcn/dot_general | solution.py:73
  70.9 14.0 %fusion.68 = f32[512,1,32]{2,1,0:T(1,128)S(1)} fusion(f32[64,512,1]{0,2,1:T(1,128)S(1)} %bitcast.113, s32[64,512]{0,1:T(8,128)S(1)} %get-tuple-element.191, s32[64,512]{0,1:T(8,128)S(1)} %get-tuple-element.192), kind=kOutput, calls=%fused_computation.8.clone.1 | convolution fusion | flops 17825792 | bytes 458752 | tf_op jit(solution)/shard_map/while/body/eval_jaxpr/eb,enb->bn/dot_general | solution.py:74
  94.9 4.5 %scatter_custom_fusion.1 = f32[2048,128]{1,0:T(8,128)} fusion(s32[1024]{0:T(1024)S(1)} %bitcast.125, f32[1024,128]{1,0:T(8,128)} %bitcast.129, f32[]{:T(128)} %constant.34.clone.1), kind=kCustom, calls=%fused_computation.92 | custom fusion | bytes 1049088 | tf_op jit(solution)/shard_map/scatter | solution.py:129
  99.4 9.8 %all-to-all-start.1 = ((f32[128,16,128]{2,1,0:T(8,128)}), f32[128,16,128]{2,1,0:T(8,128)S(1)}, u32[]{:S(2)}, u32[]{:S(2)}) async-start(f32[128,16,128]{2,1,0:T(8,128)} %bitcast.36), calls=%async_computation.1 | async-start | bytes 2097152 | tf_op jit(solution)/shard_map/all_to_all | solution.py:131
  110.6 17.9 %all-to-all-done.1 = f32[128,16,128]{2,1,0:T(8,128)S(1)} async-done(((f32[128,16,128]{2,1,0:T(8,128)}), f32[128,16,128]{2,1,0:T(8,128)S(1)}, u32[]{:S(2)}, u32[]{:S(2)}) %all-to-all-start.1) | async-done | bytes 1048608 | tf_op jit(solution)/shard_map/all_to_all | solution.py:131
  128.5 11.6 %scatter_custom_fusion.2 = f32[1025,128]{1,0:T(8,128)S(1)} fusion(s32[2048]{0:T(1024)S(1)} %bitcast.128, f32[2048,128]{1,0:T(8,128)S(1)} %bitcast.120, f32[]{:T(128)} %constant.34.clone.1), kind=kCustom, calls=%fused_computation.98 | custom fusion | flops 262144 | bytes 524804 | tf_op jit(solution)/shard_map/scatter-add | solution.py:149
  141.4 1.6 copy.50
  147.0 1.9 collective-permute-done
  149.0 2.4 collective-permute-done.1
  151.4 1.5 fusion.27
  153.1 5.2 %collective-permute-start.3 = (f32[4,1,32,256]{3,2,1,0:T(8,128)S(1)}, f32[4,1,32,256]{3,2,1,0:T(8,128)S(1)}, u32[]{:S(2)}, u32[]{:S(2)}) collective-permute-start(f32[4,1,32,256]{3,2,1,0:T(8,128)S(1)} %get-tuple-element.122), channel_id=1, source_target_pairs={{1,0},{2,1},{3,2},{4,3},{5,4},{6,5},{7,6},{8,7},{9,8},{10,9},{11,1... | collective-permute-start | bytes 393224 | tf_op jit(solution)/shard_map/ppermute | solution.py:24
  159.8 8.8 %collective-permute-start.5 = (f32[4,1,32,256]{3,2,1,0:T(8,128)S(1)}, f32[4,1,32,256]{3,2,1,0:T(8,128)S(1)}, u32[]{:S(2)}, u32[]{:S(2)}) collective-permute-start(f32[4,1,32,256]{3,2,1,0:T(8,128)S(1)} %get-tuple-element.120), channel_id=1, source_target_pairs={{1,0},{2,1},{3,2},{4,3},{5,4},{6,5},{7,6},{8,7},{9,8},{10,9},{11,1... | collective-permute-start | bytes 393224 | tf_op jit(solution)/shard_map/ppermute | solution.py:24
  170.9 1.6 reshape.162
  175.2 7.6 %gather_fusion = f32[2048,128]{1,0:T(8,128)} fusion(f32[1024,128]{1,0:T(8,128)S(1)} %copy.52, s32[2048]{0:T(1024)S(1)} %broadcast_clamp_fusion), kind=kCustom, calls=%fused_computation | custom fusion | bytes 2105344 | tf_op jit(solution)/shard_map/gather | solution.py:172
  182.8 16.9 %all-to-all-start.2 = ((f32[128,16,128]{2,1,0:T(8,128)}), f32[128,16,128]{2,1,0:T(8,128)S(1)}, u32[]{:S(2)}, u32[]{:S(2)}) async-start(f32[128,16,128]{2,1,0:T(8,128)} %bitcast.41), calls=%async_computation.2 | async-start | bytes 2097152 | tf_op jit(solution)/shard_map/all_to_all | solution.py:173
  199.8 19.3 %all-to-all-done.2 = f32[128,16,128]{2,1,0:T(8,128)S(1)} async-done(((f32[128,16,128]{2,1,0:T(8,128)}), f32[128,16,128]{2,1,0:T(8,128)S(1)}, u32[]{:S(2)}, u32[]{:S(2)}) %all-to-all-start.2) | async-done | bytes 1048608 | tf_op jit(solution)/shard_map/all_to_all | solution.py:173
  219.1 4.0 %gather_fusion.1 = f32[1024,128]{1,0:T(8,128)} fusion(f32[2048,128]{1,0:T(8,128)S(1)} %bitcast.110, s32[1024]{0:T(1024)S(1)} %broadcast_clamp_fusion.1), kind=kCustom, calls=%fused_computation.1 | custom fusion | bytes 1052672 | tf_op jit(solution)/shard_map/gather | solution.py:180
  223.1 2.1 reshape.212
  225.2 41.4 %while.21 = (s32[]{:T(128)}, f32[2,64,512]{1,2,0:T(8,128)}, f32[2,3,64,512]{2,1,3,0:T(4,128)}, s32[2,2,64,512]{2,3,1,0:T(8,128)S(1)}, f32[2,512,4,32]{3,2,1,0:T(4,128)S(1)}, /*index=5*/s32[]{:T(128)}, s32[]{:T(128)}, s32[]{}) while((s32[]{:T(128)}, f32[2,64,512]{1,2,0:T(8,128)}, f32[2,3,64,512]{2,1,3,0:T(4,128)}, ...), condition=%wide.region_10.11_spmd, body=%wide.region_8.10_spmd.sunk | while | flops 61046784 | bytes 6685325 | solution.py:104
  225.6 1.4 copy-done.1
  227.0 9.2 %fusion.72 = f32[64,512]{0,1:T(8,128)S(1)} fusion(s32[64,512]{0,1:T(8,128)S(1)} %get-tuple-element.199, s32[64,512]{0,1:T(8,128)S(1)} %get-tuple-element.200, f32[512,4,32]{2,1,0:T(4,128)S(1)} %dynamic-slice_bitcast_fusion.10, f32[2,3,64,512]{2,1,3,0:T(4,128)S(1)} %copy-done.1, s32[]{:T(128)} %get-tuple-element.233), kind=kOutput, calls=%fused_computation.37.clone.1 | convolution fusion | flops 43155456 | bytes 1048580 | tf_op jit(solution)/shard_map/while/body/eval_jaxpr/bcn,enb->ceb/dot_general | solution.py:96
  236.2 9.1 %fusion.71 = f32[512,1,64]{2,1,0:T(1,128)S(1)} fusion(s32[64,512]{0,1:T(8,128)S(1)} %get-tuple-element.199, s32[64,512]{0,1:T(8,128)S(1)} %get-tuple-element.200, f32[512,4,32]{2,1,0:T(4,128)S(1)} %dynamic-slice_bitcast_fusion.10), kind=kOutput, calls=%fused_computation.28.clone.1 | convolution fusion | flops 17825792 | bytes 917504 | tf_op jit(solution)/shard_map/while/body/eval_jaxpr/bn,enb->eb/dot_general | solution.py:99
  246.2 1.5 copy-done.1
  247.6 9.2 %fusion.72 = f32[64,512]{0,1:T(8,128)S(1)} fusion(s32[64,512]{0,1:T(8,128)S(1)} %get-tuple-element.199, s32[64,512]{0,1:T(8,128)S(1)} %get-tuple-element.200, f32[512,4,32]{2,1,0:T(4,128)S(1)} %dynamic-slice_bitcast_fusion.10, f32[2,3,64,512]{2,1,3,0:T(4,128)S(1)} %copy-done.1, s32[]{:T(128)} %get-tuple-element.233), kind=kOutput, calls=%fused_computation.37.clone.1 | convolution fusion | flops 43155456 | bytes 1048580 | tf_op jit(solution)/shard_map/while/body/eval_jaxpr/bcn,enb->ceb/dot_general | solution.py:96
  256.8 9.1 %fusion.71 = f32[512,1,64]{2,1,0:T(1,128)S(1)} fusion(s32[64,512]{0,1:T(8,128)S(1)} %get-tuple-element.199, s32[64,512]{0,1:T(8,128)S(1)} %get-tuple-element.200, f32[512,4,32]{2,1,0:T(4,128)S(1)} %dynamic-slice_bitcast_fusion.10), kind=kOutput, calls=%fused_computation.28.clone.1 | convolution fusion | flops 17825792 | bytes 917504 | tf_op jit(solution)/shard_map/while/body/eval_jaxpr/bn,enb->eb/dot_general | solution.py:99
  267.8 1.7 multiply_add_fusion.1
  (101 shorter events, 25.1 us)
Async XLA Ops:
  0.0 1.3 copy-start.6
  0.0 18.4 %copy-start.4 = (f32[3,64,1024]{2,1,0:T(8,128)S(1)}, f32[3,64,1024]{2,1,0:T(8,128)}, u32[]{:S(2)}) copy-start(f32[3,64,1024]{2,1,0:T(8,128)} %param.13) | copy-start | bytes 2359300
  1.2 19.0 %copy-start.5 = (s32[2,64,1024]{2,1,0:T(8,128)S(1)}, s32[2,64,1024]{2,1,0:T(8,128)}, u32[]{:S(2)}) copy-start(s32[2,64,1024]{2,1,0:T(8,128)} %param.15) | copy-start | bytes 1572868
  1.7 93.2 %copy-start.7 = (s32[1024,1]{0,1:T(1,128)}, s32[1024,1]{0,1:T(1,128)S(1)}, u32[]{:S(2)}) copy-start(s32[1024,1]{0,1:T(1,128)S(1)} %compare_select_fusion.2) | copy-start | bytes 12292
  6.9 92.5 %all-to-all-start = ((s32[128,1,16]{2,1,0:T(1,128)}), s32[128,1,16]{2,1,0:T(1,128)S(1)}, u32[]{:S(2)}, u32[]{:S(2)}) async-start(s32[128,1,16]{2,1,0:T(1,128)} %bitcast.30), calls=%async_computation | async-start | bytes 131072 | tf_op jit(solution)/shard_map/all_to_all | solution.py:138
  18.4 2.6 copy-start.3
  39.0 14.3 %copy-start.14 = (f32[2,512,128]{2,1,0:T(8,128)S(1)}, f32[2,512,128]{2,1,0:T(8,128)}, u32[]{:S(2)}) copy-start(f32[2,512,128]{2,1,0:T(8,128)} %get-tuple-element.210) | copy-start | bytes 1572868 | tf_op jit(solution)/shard_map/while
  53.4 0.8 copy-start.15
  70.9 14.3 %copy-start.14 = (f32[2,512,128]{2,1,0:T(8,128)S(1)}, f32[2,512,128]{2,1,0:T(8,128)}, u32[]{:S(2)}) copy-start(f32[2,512,128]{2,1,0:T(8,128)} %get-tuple-element.210) | copy-start | bytes 1572868 | tf_op jit(solution)/shard_map/while
  85.3 0.8 copy-start.15
  99.4 29.1 %all-to-all-start.1 = ((f32[128,16,128]{2,1,0:T(8,128)}), f32[128,16,128]{2,1,0:T(8,128)S(1)}, u32[]{:S(2)}, u32[]{:S(2)}) async-start(f32[128,16,128]{2,1,0:T(8,128)} %bitcast.36), calls=%async_computation.1 | async-start | bytes 2097152 | tf_op jit(solution)/shard_map/all_to_all | solution.py:131
  143.1 8.3 %copy-start.2 = (f32[4,32,256]{2,1,0:T(8,128)S(1)}, f32[4,32,256]{2,1,0:T(8,128)}, u32[]{:S(2)}) copy-start(f32[4,32,256]{2,1,0:T(8,128)} %param.18) | copy-start | bytes 393220
  143.1 8.3 %copy-start.9 = (f32[4]{0:T(128)S(1)}, f32[4]{0:T(128)}, u32[]{:S(2)}) copy-start(f32[4]{0:T(128)} %constant.74.clone) | copy-start | bytes 52
  143.1 8.3 %copy-start.11 = (f32[4]{0:T(128)S(1)}, f32[4]{0:T(128)}, u32[]{:S(2)}) copy-start(f32[4]{0:T(128)} %constant.96) | copy-start | bytes 52
  144.5 14.7 %copy-start = (f32[4,4,32,256]{3,2,1,0:T(8,128)S(1)}, f32[4,4,32,256]{3,2,1,0:T(8,128)}, u32[]{:S(2)}) copy-start(f32[4,4,32,256]{3,2,1,0:T(8,128)} %reshape.161) | copy-start | bytes 1572868
  144.5 14.7 %copy-start.13 = (f32[4]{0:T(128)S(1)}, f32[4]{0:T(128)}, u32[]{:S(2)}) copy-start(f32[4]{0:T(128)} %constant.97) | copy-start | bytes 52
  145.8 3.2 %collective-permute-start = (f32[4,1,32,256]{3,2,1,0:T(8,128)S(1)}, f32[4,1,32,256]{3,2,1,0:T(8,128)S(1)}, u32[]{:S(2)}, u32[]{:S(2)}) collective-permute-start(f32[4,1,32,256]{3,2,1,0:T(8,128)S(1)} %get-tuple-element.123), channel_id=1, source_target_pairs={{0,1},{1,2},{2,3},{3,4},{4,5},{5,6},{6,7},{7,8},{8,9},{9,10},{10,1... | collective-permute-start | bytes 393224 | tf_op jit(solution)/shard_map/ppermute | solution.py:22
  147.0 4.4 %collective-permute-start.1 = (f32[4,1,32,256]{3,2,1,0:T(8,128)S(1)}, f32[4,1,32,256]{3,2,1,0:T(8,128)S(1)}, u32[]{:S(2)}, u32[]{:S(2)}) collective-permute-start(f32[4,1,32,256]{3,2,1,0:T(8,128)S(1)} %get-tuple-element.124), channel_id=1, source_target_pairs={{1,0},{2,1},{3,2},{4,3},{5,4},{6,5},{7,6},{8,7},{9,8},{10,9},{11,1... | collective-permute-start | bytes 393224 | tf_op jit(solution)/shard_map/ppermute | solution.py:24
  152.9 16.7 %copy-start.10 = (f32[4]{0:T(128)S(1)}, f32[4]{0:T(128)}, u32[]{:S(2)}) copy-start(f32[4]{0:T(128)} %constant.74.clone) | copy-start | bytes 52
  152.9 16.7 %copy-start.12 = (f32[4]{0:T(128)S(1)}, f32[4]{0:T(128)}, u32[]{:S(2)}) copy-start(f32[4]{0:T(128)} %constant.96) | copy-start | bytes 52
  153.0 6.0 %collective-permute-start.2 = (f32[4,1,32,256]{3,2,1,0:T(8,128)S(1)}, f32[4,1,32,256]{3,2,1,0:T(8,128)S(1)}, u32[]{:S(2)}, u32[]{:S(2)}) collective-permute-start(f32[4,1,32,256]{3,2,1,0:T(8,128)S(1)} %get-tuple-element.121), channel_id=1, source_target_pairs={{0,1},{1,2},{2,3},{3,4},{4,5},{5,6},{6,7},{7,8},{8,9},{9,10},{10,1... | collective-permute-start | bytes 393224 | tf_op jit(solution)/shard_map/ppermute | solution.py:22
  153.1 6.1 %collective-permute-start.3 = (f32[4,1,32,256]{3,2,1,0:T(8,128)S(1)}, f32[4,1,32,256]{3,2,1,0:T(8,128)S(1)}, u32[]{:S(2)}, u32[]{:S(2)}) collective-permute-start(f32[4,1,32,256]{3,2,1,0:T(8,128)S(1)} %get-tuple-element.122), channel_id=1, source_target_pairs={{1,0},{2,1},{3,2},{4,3},{5,4},{6,5},{7,6},{8,7},{9,8},{10,9},{11,1... | collective-permute-start | bytes 393224 | tf_op jit(solution)/shard_map/ppermute | solution.py:24
  159.7 9.7 %collective-permute-start.4 = (f32[4,1,32,256]{3,2,1,0:T(8,128)S(1)}, f32[4,1,32,256]{3,2,1,0:T(8,128)S(1)}, u32[]{:S(2)}, u32[]{:S(2)}) collective-permute-start(f32[4,1,32,256]{3,2,1,0:T(8,128)S(1)} %get-tuple-element.119), channel_id=1, source_target_pairs={{0,1},{1,2},{2,3},{3,4},{4,5},{5,6},{6,7},{7,8},{8,9},{9,10},{10,1... | collective-permute-start | bytes 393224 | tf_op jit(solution)/shard_map/ppermute | solution.py:22
  159.8 9.8 %collective-permute-start.5 = (f32[4,1,32,256]{3,2,1,0:T(8,128)S(1)}, f32[4,1,32,256]{3,2,1,0:T(8,128)S(1)}, u32[]{:S(2)}, u32[]{:S(2)}) collective-permute-start(f32[4,1,32,256]{3,2,1,0:T(8,128)S(1)} %get-tuple-element.120), channel_id=1, source_target_pairs={{1,0},{2,1},{3,2},{4,3},{5,4},{6,5},{7,6},{8,7},{9,8},{10,9},{11,1... | collective-permute-start | bytes 393224 | tf_op jit(solution)/shard_map/ppermute | solution.py:24
  182.8 17.0 %copy-start.8 = (s32[1024,1]{0,1:T(1,128)S(1)}, s32[1024,1]{0,1:T(1,128)}, u32[]{:S(2)}) copy-start(s32[1024,1]{0,1:T(1,128)} %copy-done.7) | copy-start | bytes 12292
  182.8 36.3 %all-to-all-start.2 = ((f32[128,16,128]{2,1,0:T(8,128)}), f32[128,16,128]{2,1,0:T(8,128)S(1)}, u32[]{:S(2)}, u32[]{:S(2)}) async-start(f32[128,16,128]{2,1,0:T(8,128)} %bitcast.41), calls=%async_computation.2 | async-start | bytes 2097152 | tf_op jit(solution)/shard_map/all_to_all | solution.py:173
  225.4 1.6 copy-start.1
  246.0 1.6 copy-start.1
where the time goes:
time: 274 us; the launch traced here: 270 us
  matrix products  95.5 us (35%)
  starting transfers between devices  53.5 us (20%)
  local copies, waits for them, and re-layouts  44.3 us (16%)
  waiting for transfers between devices  43.6 us (16%)
  other arithmetic  22.8 us (8%)
  loops' own time  9.38 us (3%)
    dot_general x2, matrix products, block_one_group(): jnp.einsum('ceb,enb->bcn', vector_part, head_hot + tail_hot, precision=hi...  30.9 us
    dot_general x2, matrix products, block_one_group(): jnp.einsum('eb,enb->bn', resid_part, head_hot - tail_hot, precision=highest)  28.1 us
    all_to_all x1, waiting for transfers between devices, per_device(): lax.all_to_all(outgoing.reshape(devices, capacity, width), ('edge', 'node...  19.3 us
    dot_general x2, matrix products, lift_one_group(): jnp.einsum('bcn,enb->ceb', value_part[:, :3], head_hot + tail_hot, precis...  18.3 us
    dot_general x2, matrix products, lift_one_group(): jnp.einsum('bn,enb->eb', value_part[:, 3], head_hot - tail_hot, precision...  18.2 us
    all_to_all x1, waiting for transfers between devices, per_device(): lax.all_to_all(partials.reshape(devices, capacity, width), ('edge', 'node...  17.9 us
    all_to_all x1, starting transfers between devices, per_device(): lax.all_to_all(outgoing.reshape(devices, capacity, width), ('edge', 'node...  16.9 us
    ppermute x3, starting transfers between devices, with_halo(): lax.ppermute(head, axis, [((i + 1) % count, i) for i in range(count)])  14 us
  transfers between devices with their start and end apart: 9, of which 8 were waited for; matrix products, arithmetic and copies ran while one was open for 27% of the time, Pallas kernels for 0%

commit v1 on v0

v1 whole, which is shorter than its diff:
```python
import jax
import jax.numpy as jnp
from jax import lax
from jax.experimental import pallas as pl
from jax.experimental.pallas import tpu as pltpu
from jax.sharding import PartitionSpec as P

F32 = jnp.float32
BF16 = jnp.bfloat16
I32 = jnp.int32

EDGES = 64
NODES = 32
ROW = 4 * NODES
BLOCKS = 1024
CAP = 16
DEVICES = 128
SLOTS = DEVICES * CAP
SLICE = 256
HALO = 3 * SLICE
LABEL = 3 * NODES
RING = ("edge", "node")
VMEM_LIMIT = 48 * 1024 * 1024

mass_scale = (1.0, 1.0, 1.0, 0.5)


def chebyshev_numbers(scale):
    upper = 12.0 + 8.0 * scale
    lower = upper / 8.0
    centre = (upper + lower) / 2.0
    radius = (upper - lower) / 2.0
    ratio = centre / radius
    first = 1.0 / ratio
    second = 1.0 / (2.0 * ratio - first)
    return (centre, second * first, 2.0 * second / radius)


def place(slab):
    return slab ^ (24 * ((slab >> 5) & 1)) ^ (6 * ((slab >> 3) & 1))


def split(value):
    high = value.astype(BF16)
    return high, (value - high.astype(F32)).astype(BF16)


def one_hot(mask):
    return jnp.where(mask, 1.0, 0.0).astype(BF16)


def iota(shape, dim):
    return lax.broadcasted_iota(I32, shape, dim)


def dot(left, right, dims):
    return lax.dot_general(left, right, (dims, ((), ())), preferred_element_type=F32)


def terms_kernel(res_ref, tan_ref, ends_ref, target_ref, block_ref, send_ref, slot_ref, term_scr, acc_scr, hot_scr):
    term_scr[...] = 0.5 * tan_ref[...] * res_ref[...][None]
    node = iota((NODES, 128), 0)

    def lanes_step(group, _):
        lanes = pl.ds(pl.multiple_of(group * 128, 128), 128)

        sums = [jnp.zeros((NODES, 128), F32)] * 4
        for number in range(EDGES):
            edge = slice(number, number + 1)
            head = ends_ref[1, edge, lanes] == node
            tail = ends_ref[0, edge, lanes] == node
            either = head | tail
            value = res_ref[edge, lanes]
            for channel in range(3):
                sums[channel] = sums[channel] + jnp.where(either, term_scr[channel, edge, lanes], 0.0)
            sums[3] = sums[3] + jnp.where(head, value, jnp.where(tail, -value, 0.0))
        for channel in range(4):
            acc_scr[channel * NODES : (channel + 1) * NODES, lanes] = sums[channel]
        return 0

    lax.fori_loop(0, BLOCKS // 128, lanes_step, 0)

    number = block_ref[...]
    label = (number & ~255) + (number & 7) * 32 + ((number >> 3) & 31)
    acc_scr[LABEL : LABEL + 1, :] = (label + 1).astype(F32)

    holder = place(target_ref[...])
    device = iota((DEVICES, 128), 0)
    before = one_hot(iota((128, 128), 0) < iota((128, 128), 1))
    seen = jnp.zeros((DEVICES, 1), F32)
    for group in range(BLOCKS // 128):
        lanes = slice(group * 128, (group + 1) * 128)
        same = holder[:, lanes] == device
        hot = jnp.where(same, 1.0, 0.0)
        count = dot(hot.astype(BF16), before, ((1,), (0,))) + seen
        rank = jnp.sum(jnp.where(same, count, 0.0), axis=0, keepdims=True)
        slot_ref[:, lanes] = holder[:, lanes] * CAP + rank.astype(I32)
        seen = seen + jnp.sum(hot, axis=1, keepdims=True)

    high, low = split(acc_scr[...])
    hot_scr[0:ROW, :] = high
    hot_scr[ROW:, :] = low
    slots = slot_ref[...]

    def send_step(step, _):
        rows = pl.ds(pl.multiple_of(step * 256, 256), 256)
        hot = one_hot(slots == iota((256, BLOCKS), 0) + step * 256)
        both = dot(hot, hot_scr[...], ((1,), (1,)))
        send_ref[rows, :] = both[:, :ROW] + both[:, ROW:]
        return 0

    lax.fori_loop(0, SLOTS // 256, send_step, 0)


def edge_terms(residual, tangent, ends, target, node_block):
    return pl.pallas_call(
        terms_kernel,
        out_shape=(
            jax.ShapeDtypeStruct((SLOTS, ROW), F32),
            jax.ShapeDtypeStruct((1, BLOCKS), I32),
        ),
        in_specs=[pl.BlockSpec(memory_space=pltpu.VMEM)] * 5,
        out_specs=[pl.BlockSpec(memory_space=pltpu.VMEM)] * 2,
        scratch_shapes=[
            pltpu.VMEM((3, EDGES, BLOCKS), F32),
            pltpu.VMEM((ROW, BLOCKS), F32),
            pltpu.VMEM((2 * ROW, BLOCKS), BF16),
        ],
        compiler_params=pltpu.CompilerParams(vmem_limit_bytes=VMEM_LIMIT),
        name="edge_terms",
    )(residual, tangent, ends, target, node_block)


def transposed_rows(rows_ref, out_scr):
    for step in range(SLOTS // 128):
        part = slice(step * 128, (step + 1) * 128)
        high, low = split(rows_ref[part, :].T)
        out_scr[0:ROW, part] = high
        out_scr[ROW:, part] = low


def sums_kernel(got_ref, own_ref, before_ref, after_ref, rows_scr, hot_scr):
    transposed_rows(got_ref, rows_scr)

    def hot_step(step, _):
        part = pl.ds(pl.multiple_of(step * 256, 256), 256)
        label = got_ref[part, LABEL : LABEL + 1].astype(I32)
        hot_scr[part, :] = one_hot(label == iota((256, BLOCKS), 1) + 1)
        return 0

    lax.fori_loop(0, SLOTS // 256, hot_step, 0)
    for step in range(BLOCKS // 256):
        lanes = slice(step * 256, (step + 1) * 256)
        both = dot(rows_scr[...], hot_scr[:, lanes], ((1,), (0,)))
        sums = both[:ROW] + both[ROW:]
        scalar = sums[LABEL:]
        first = iota((NODES, 256), 0) == 0
        rest = -jnp.sum(jnp.where(first, 0.0, scalar), axis=0, keepdims=True)
        own_ref[0:LABEL, lanes] = sums[:LABEL]
        own_ref[LABEL:, lanes] = jnp.where(first, rest, scalar)
    before_ref[...] = own_ref[:, 0:HALO]
    after_ref[...] = own_ref[:, BLOCKS - HALO :]


def block_sums(got):
    return pl.pallas_call(
        sums_kernel,
        out_shape=(
            jax.ShapeDtypeStruct((ROW, BLOCKS), F32),
            jax.ShapeDtypeStruct((ROW, HALO), F32),
            jax.ShapeDtypeStruct((ROW, HALO), F32),
        ),
        in_specs=[pl.BlockSpec(memory_space=pltpu.VMEM)],
        out_specs=[pl.BlockSpec(memory_space=pltpu.VMEM)] * 3,
        scratch_shapes=[
            pltpu.VMEM((2 * ROW, SLOTS), BF16),
            pltpu.VMEM((SLOTS, BLOCKS), BF16),
        ],
        compiler_params=pltpu.CompilerParams(vmem_limit_bytes=VMEM_LIMIT),
        name="block_sums",
    )(got)


def beside(field):
    row = iota((8, SLICE), 0)
    lane = iota((8, SLICE), 1)
    up = pltpu.roll(field, 1, 0)
    edge = up[0:8]
    wrap = jnp.where(lane >= 32, pltpu.roll(edge, 32, 1), 0.0)
    up = jnp.concatenate([jnp.where(row == 0, wrap, edge), up[8:]], axis=0)
    down = pltpu.roll(field, NODES - 1, 0)
    edge = down[24:32]
    wrap = jnp.where(lane < SLICE - 32, pltpu.roll(edge, SLICE - 32, 1), 0.0)
    down = jnp.concatenate([down[:24], jnp.where(row == 7, wrap, edge)], axis=0)
    radial = iota((NODES, SLICE), 1) & 31
    inner = jnp.where(radial > 0, pltpu.roll(field, 1, 1), 0.0)
    outer = jnp.where(radial < 31, pltpu.roll(field, SLICE - 1, 1), 0.0)
    return (up + down) + (inner + outer)


def sweeps_kernel(own_ref, prev_ref, next_ref, got_ref, sig_own_ref, sig_prev_ref, sig_next_ref, back_ref, sig_scr, y_scr, d_scr, sol_scr):
    for first, count, ref in ((0, 2, sig_prev_ref), (2, 4, sig_own_ref), (6, 2, sig_next_ref)):
        for s in range(count):
            turned = ref[s].T
            for block in range(8):
                at = (first + s) * SLICE + block * 32
                sig_scr[:, at : at + 32] = turned[block * 32 : (block + 1) * 32, :]

    def channel_step(channel, _):
        scalar = channel == 3
        vector_numbers = chebyshev_numbers(mass_scale[0])
        scalar_numbers = chebyshev_numbers(mass_scale[3])
        centre, one, two = [
            jnp.where(scalar, b, a).astype(F32) for a, b in zip(vector_numbers, scalar_numbers)
        ]
        mass = jnp.where(scalar, mass_scale[3], mass_scale[0]).astype(F32)
        invert = jnp.where(scalar, 1.0 / scalar_numbers[0], 1.0 / vector_numbers[0]).astype(F32)
        rows = pl.ds(pl.multiple_of(channel * NODES, NODES), NODES)

        def source(s):
            if s < 0:
                return prev_ref[rows, (s + 3) * SLICE : (s + 4) * SLICE]
            if s > 3:
                return next_ref[rows, (s - 4) * SLICE : (s - 3) * SLICE]
            return own_ref[rows, s * SLICE : (s + 1) * SLICE]

        def diag(s):
            return 6.0 + mass * sig_scr[:, (s + 2) * SLICE : (s + 3) * SLICE]

        def held(scr, s):
            return scr[:, (s + 2) * SLICE : (s + 3) * SLICE]

        for s in range(-2, 6):
            here = source(s) * invert
            applied = diag(s) * here - ((source(s - 1) + source(s + 1)) * invert + beside(here))
            rest = source(s) - applied
            y_scr[:, (s + 2) * SLICE : (s + 3) * SLICE] = here + (one * here + two * rest)
        for s in range(-1, 5):
            here = held(y_scr, s)
            applied = diag(s) * here - ((held(y_scr, s - 1) + held(y_scr, s + 1)) + beside(here))
            d_scr[:, (s + 2) * SLICE : (s + 3) * SLICE] = source(s) - applied
        for s in range(0, 4):
            rest = held(d_scr, s)
            here = rest * invert
            applied = diag(s) * here - ((held(d_scr, s - 1) + held(d_scr, s + 1)) * invert + beside(here))
            rest = rest - applied
            value = (held(y_scr, s) + here) + (one * here + two * rest)
            high, low = split(value)
            lanes = slice(s * SLICE, (s + 1) * SLICE)
            sol_scr[rows, lanes] = high
            sol_scr[pl.ds(pl.multiple_of(ROW + channel * NODES, NODES), NODES), lanes] = low
        return 0

    lax.fori_loop(0, 4, channel_step, 0)

    def back_step(step, _):
        part = pl.ds(pl.multiple_of(step * 256, 256), 256)
        label = got_ref[part, LABEL : LABEL + 1].astype(I32)
        hot = one_hot(label == iota((256, BLOCKS), 1) + 1)
        both = dot(hot, sol_scr[...], ((1,), (1,)))
        back_ref[part, :] = both[:, :ROW] + both[:, ROW:]
        return 0

    lax.fori_loop(0, SLOTS // 256, back_step, 0)


def sweeps(own, prev_part, next_part, got, sig_own, sig_prev, sig_next):
    return pl.pallas_call(
        sweeps_kernel,
        out_shape=jax.ShapeDtypeStruct((SLOTS, ROW), F32),
        in_specs=[pl.BlockSpec(memory_space=pltpu.VMEM)] * 7,
        out_specs=pl.BlockSpec(memory_space=pltpu.VMEM),
        scratch_shapes=[
            pltpu.VMEM((NODES, 8 * SLICE), F32),
            pltpu.VMEM((NODES, 8 * SLICE), F32),
            pltpu.VMEM((NODES, 8 * SLICE), F32),
            pltpu.VMEM((2 * ROW, BLOCKS), BF16),
        ],
        compiler_params=pltpu.CompilerParams(vmem_limit_bytes=VMEM_LIMIT),
        name="sweeps",
    )(own, prev_part, next_part, got, sig_own, sig_prev, sig_next)


def lift_kernel(got_ref, slot_ref, res_ref, tan_ref, jac_ref, ends_ref, out_ref, rows_scr, hot_scr, y_scr):
    transposed_rows(got_ref, rows_scr)
    slots = slot_ref[...]

    def hot_step(step, _):
        part = pl.ds(pl.multiple_of(step * 256, 256), 256)
        hot_scr[part, :] = one_hot(slots == iota((256, BLOCKS), 0) + step * 256)
        return 0

    lax.fori_loop(0, SLOTS // 256, hot_step, 0)
    for step in range(BLOCKS // 256):
        lanes = slice(step * 256, (step + 1) * 256)
        both = dot(rows_scr[...], hot_scr[:, lanes], ((1,), (0,)))
        y_scr[:, lanes] = both[:ROW] + both[ROW:]

    def lanes_step(group, _):
        lanes = pl.ds(pl.multiple_of(group * 128, 128), 128)

        def pick(channel, low, quarter):
            parts = [
                jnp.take_along_axis(y_scr[channel * NODES + 8 * k : channel * NODES + 8 * k + 8, lanes], low, axis=0)
                for k in range(4)
            ]
            return jnp.where(
                quarter < 2,
                jnp.where(quarter == 0, parts[0], parts[1]),
                jnp.where(quarter == 2, parts[2], parts[3]),
            )

        for step in range(EDGES // 8):
            edges = slice(step * 8, (step + 1) * 8)
            tail = ends_ref[0, edges, lanes]
            head = ends_ref[1, edges, lanes]
            tail_at = (tail & 7, tail >> 3)
            head_at = (head & 7, head >> 3)
            total = pick(3, *head_at) - pick(3, *tail_at)
            for channel in range(3):
                pair = pick(channel, *head_at) + pick(channel, *tail_at)
                total = total + 0.5 * tan_ref[channel, edges, lanes] * pair
            out_ref[edges, lanes] = jac_ref[edges, lanes] * res_ref[edges, lanes] + total
        return 0

    lax.fori_loop(0, BLOCKS // 128, lanes_step, 0)


def lift(got, slots, residual, tangent, jacobi, ends):
    return pl.pallas_call(
        lift_kernel,
        out_shape=jax.ShapeDtypeStruct((EDGES, BLOCKS), F32),
        in_specs=[pl.BlockSpec(memory_space=pltpu.VMEM)] * 6,
        out_specs=pl.BlockSpec(memory_space=pltpu.VMEM),
        scratch_shapes=[
            pltpu.VMEM((2 * ROW, SLOTS), BF16),
            pltpu.VMEM((SLOTS, BLOCKS), BF16),
            pltpu.VMEM((ROW, BLOCKS), F32),
        ],
        compiler_params=pltpu.CompilerParams(vmem_limit_bytes=VMEM_LIMIT),
        name="lift",
    )(got, slots, residual, tangent, jacobi, ends)


def exchange(rows):
    parts = rows.reshape(DEVICES, CAP, ROW)
    return lax.all_to_all(parts, RING, split_axis=0, concat_axis=0, tiled=True).reshape(SLOTS, ROW)


def per_device(residual, tangent, jacobi, ends, target, node_block, sigma):
    slabs = range(DEVICES)
    forward = [(place(s), place((s + 1) % DEVICES)) for s in slabs]
    backward = [(place((s + 1) % DEVICES), place(s)) for s in slabs]
    sig_own = lax.ppermute(sigma, RING, [(s, place(s)) for s in slabs])
    sig_prev = lax.ppermute(sigma[2:], RING, [(s, place((s + 1) % DEVICES)) for s in slabs])
    sig_next = lax.ppermute(sigma[:2], RING, [((s + 1) % DEVICES, place(s)) for s in slabs])
    send, slots = edge_terms(
        residual, tangent, ends, target.reshape(1, BLOCKS), node_block.reshape(1, BLOCKS)
    )
    got = exchange(send)
    own, to_prev, to_next = block_sums(got)
    prev_part = lax.ppermute(to_next, RING, forward)
    next_part = lax.ppermute(to_prev, RING, backward)
    back = sweeps(own, prev_part, next_part, got, sig_own, sig_prev, sig_next)
    mine = exchange(back)
    return lift(mine, slots, residual, tangent, jacobi, ends)


def solution(mesh):
    in_specs = (
        P(None, RING),
        P(None, None, RING),
        P(None, RING),
        P(None, None, RING),
        P(RING, None),
        P(RING),
        P(RING, None, None),
    )
    return jax.shard_map(
        per_device, mesh=mesh, in_specs=in_specs, out_specs=P(None, RING), check_vma=False
    )
```

time: 274 us -> 97 us (0.35); the launches traced: 270 us -> 96.7 us
  matrix products: 95.5 us -> 0 us
  blocking collectives: 0 us -> 61.2 us
  starting transfers between devices: 53.5 us -> 4.63 us
  local copies, waits for them, and re-layouts: 44.3 us -> 4.54 us
  waiting for transfers between devices: 43.6 us -> 4.38 us
  other arithmetic: 22.8 us -> 0 us
  Pallas kernels: 0 us -> 21.9 us
  loops' own time: 9.38 us -> 0 us
    dot_general x8 -> x0, matrix products: 95.5 us -> none  [the longest x2 30.9 us: block_one_group(): jnp.einsum('ceb,enb->bcn', vector_part, head_hot + tail_hot, precision=hi...]
    all_to_all x0 -> x2, blocking collectives: none -> 61.2 us  [exchange(): lax.all_to_all(parts, RING, split_axis=0, concat_axis=0, tiled=True)]
    all_to_all x3 -> x0, starting transfers between devices: 38.2 us -> none  [the longest x1 16.9 us: per_device(): lax.all_to_all(outgoing.reshape(devices, capacity, width), ('edge', 'node...]
    all_to_all x3 -> x0, waiting for transfers between devices: 37.2 us -> none  [the longest x1 19.3 us: per_device(): lax.all_to_all(outgoing.reshape(devices, capacity, width), ('edge', 'node...]
    pallas_call x0 -> x4, Pallas kernels: none -> 21.9 us  [the longest x1 9.55 us: edge_terms(): pl.pallas_call(terms_kernel, out_shape=(jax.ShapeDtypeStruct((SLOTS, ROW)...]
    scatter-add x1 -> x0, other arithmetic: 11.6 us -> none  [per_device(): jax.ops.segment_sum(got_terms, safe_labels, num_segments=nodal_blocks + 1)]
    gather x2 -> x0, local copies, waits for them, and re-layouts: 11.6 us -> none  [the longest x1 7.6 us: per_device(): outgoing = sol_blocks[jnp.clip(got_labels, 0, nodal_blocks - 1)]]
    ppermute x6 -> x5, starting transfers between devices: 15.4 us -> 4.63 us  [the longest x1 2.84 us: per_device(): lax.ppermute(sigma[:2], RING, [((s + 1) % DEVICES, place(s)) for s in sla...]
  transfers between devices with their start and end apart: 9 -> 5, of which waited for: 8 -> 1; matrix products, arithmetic and copies ran while one was open for 27% -> 0% of each run, Pallas kernels for 0% -> 0%
where the time goes in v1:
time: 97 us; the launch traced here: 96.7 us
  blocking collectives  61.2 us (63%)
  Pallas kernels  21.9 us (23%)
  starting transfers between devices  4.63 us (5%)
  local copies, waits for them, and re-layouts  4.54 us (5%)
  waiting for transfers between devices  4.38 us (5%)
    all_to_all x2, blocking collectives, exchange(): lax.all_to_all(parts, RING, split_axis=0, concat_axis=0, tiled=True)  61.2 us
    pallas_call x1, Pallas kernels, edge_terms(): pl.pallas_call(terms_kernel, out_shape=(jax.ShapeDtypeStruct((SLOTS, ROW)...  9.55 us
    pallas_call x1, Pallas kernels, sweeps(): pl.pallas_call(sweeps_kernel, out_shape=jax.ShapeDtypeStruct((SLOTS, ROW)...  5.6 us
    unnamed x20, local copies, waits for them, and re-layouts  4.52 us
    ppermute x1, waiting for transfers between devices, per_device(): lax.ppermute(sigma[:2], RING, [((s + 1) % DEVICES, place(s)) for s in sla...  4.37 us
    pallas_call x1, Pallas kernels, lift(): pl.pallas_call(lift_kernel, out_shape=jax.ShapeDtypeStruct((EDGES, BLOCKS...  3.88 us
    pallas_call x1, Pallas kernels, block_sums(): pl.pallas_call(sums_kernel, out_shape=(jax.ShapeDtypeStruct((ROW, BLOCKS)...  2.85 us
    ppermute x1, starting transfers between devices, per_device(): lax.ppermute(sigma[:2], RING, [((s + 1) % DEVICES, place(s)) for s in sla...  2.84 us
  transfers between devices with their start and end apart: 5, of which 1 were waited for; matrix products, arithmetic and copies ran while one was open for 0% of the time, Pallas kernels for 0%

profile of v1, /device:TPU:1, one launch (start us, length us, event | category | flops | bytes accessed | tf_op | source)
XLA Modules:
  0.0 96.7 jit_solution(17090989994993193392)
XLA Ops:
  0.0 1.1 %copy-done = f32[3,64,1024]{2,1,0:T(8,128)S(1)} copy-done((f32[3,64,1024]{2,1,0:T(8,128)S(1)}, f32[3,64,1024]{2,1,0:T(8,128)}, u32[]{:S(2)}) %copy-start) | copy-done | bytes 786456
  1.1 0.0 copy-start.2
  1.1 1.0 %copy-done.2 = s32[2,64,1024]{2,1,0:T(8,128)S(1)} copy-done((s32[2,64,1024]{2,1,0:T(8,128)S(1)}, s32[2,64,1024]{2,1,0:T(8,128)}, u32[]{:S(2)}) %copy-start.2) | copy-done | bytes 524312
  2.2 0.0 copy-start.4
  2.2 0.9 copy-done.4
  3.1 0.7 copy-done.7
  3.8 0.7 copy-done.8
  4.5 9.5 %edge_terms.1 = (f32[2048,128]{1,0:T(8,128)S(1)}, s32[1,1024]{1,0:T(1,128)S(1)}) custom-call(f32[64,1024]{1,0:T(8,128)S(1)} %copy-done.4, f32[3,64,1024]{2,1,0:T(8,128)S(1)} %copy-done, s32[2,64,1024]{2,1,0:T(8,128)S(1)} %copy-done.2, s32[1,1024]{1,0:T(1,128)S(1)} %bitcast.11, s32[1,1024]{1,0:T(1,128)S(1)} %bitcast.12), custom_call_target="tpu_custom_call" | custom-call | tf_op jit(solution)/shard_map/edge_terms/pallas_call | solution.py:116
  14.1 30.6 %all_to_all.10 = f32[128,16,128]{2,1,0:T(8,128)S(1)} all-to-all(f32[128,16,128]{2,1,0:T(8,128)S(1)} %bitcast.10), channel_id=1, replica_groups=mesh['edge'=16,'node'=8] {'edge','node'}, dimensions={0} | all-to-all | bytes 2097152 | tf_op jit(solution)/shard_map/all_to_all | solution.py:347
  44.7 2.9 %block_sums.1 = (f32[128,1024]{1,0:T(8,128)S(1)}, f32[128,768]{1,0:T(8,128)S(1)}, f32[128,768]{1,0:T(8,128)S(1)}) custom-call(f32[2048,128]{1,0:T(8,128)S(1)} %bitcast.6), custom_call_target="tpu_custom_call" | custom-call | tf_op jit(solution)/shard_map/block_sums/pallas_call | solution.py:166
  47.6 1.1 %collective-permute-start = (f32[128,768]{1,0:T(8,128)S(1)}, f32[128,768]{1,0:T(8,128)S(1)}, u32[]{:S(2)}, u32[]{:S(2)}) collective-permute-start(f32[128,768]{1,0:T(8,128)S(1)} %get-tuple-element.12), channel_id=1, source_target_pairs={{0,1},{1,2},{2,3},{3,4},{4,5},{5,6},{6,7},{7,14},{14,15},{15,12},{... | collective-permute-start | bytes 1179656 | tf_op jit(solution)/shard_map/ppermute | solution.py:362
  48.7 0.0 collective-permute-start.1
  48.7 0.0 copy-done.9
  48.7 0.7 collective-permute-start.2
  49.4 2.8 %collective-permute-start.4 = (f32[2,32,256]{2,1,0:T(8,128)S(1)}, f32[2,32,256]{2,1,0:T(8,128)S(1)}, u32[]{:S(2)}, u32[]{:S(2)}) collective-permute-start(f32[2,32,256]{2,1,0:T(8,128)S(1)} %get-tuple-element.15), channel_id=1, source_target_pairs={{1,0},{2,1},{3,2},{4,3},{5,4},{6,5},{7,6},{8,7},{9,14},{10,15},{11... | collective-permute-start | bytes 196616 | tf_op jit(solution)/shard_map/ppermute | solution.py:356
  52.2 0.0 collective-permute-start.3
  52.2 4.4 %collective-permute-done.4.sig_next_ref = f32[2,32,256]{2,1,0:T(8,128)S(1)} collective-permute-done((f32[2,32,256]{2,1,0:T(8,128)S(1)}, f32[2,32,256]{2,1,0:T(8,128)S(1)}, u32[]{:S(2)}, u32[]{:S(2)}) %collective-permute-start.4) | collective-permute-done | bytes 65568 | tf_op jit(solution)/shard_map/ppermute | solution.py:356
  56.6 0.0 collective-permute-done.3.sig_prev_ref
  56.6 0.0 collective-permute-done.2.sig_own_ref
  56.6 0.0 collective-permute-done.prev_ref
  56.6 0.0 collective-permute-done.1.next_ref
  56.6 5.6 %sweeps.1 = f32[2048,128]{1,0:T(8,128)S(1)} custom-call(f32[128,1024]{1,0:T(8,128)S(1)} %get-tuple-element.11.own_ref, f32[128,768]{1,0:T(8,128)S(1)} %collective-permute-done.prev_ref, f32[128,768]{1,0:T(8,128)S(1)} %collective-permute-done.1.next_ref, f32[2048,128]{1,0:T(8,128)S(1)} %bitcast.7, f32[4,32,256]{2,1,0:T(8,128)S(1)} %collective-permute-done.2.sig_own_ref, ...), custom_call_target="tpu_custom_call" | custom-call | tf_op jit(solution)/shard_map/sweeps/pallas_call | solution.py:268
  62.2 0.0 copy-start.1
  62.2 0.0 copy-start.3
  62.2 0.0 copy-start.5
  62.3 0.0 copy-start.6
  62.3 30.5 %all_to_all.11 = f32[128,16,128]{2,1,0:T(8,128)S(1)} all-to-all(f32[128,16,128]{2,1,0:T(8,128)S(1)} %bitcast.8), channel_id=1, replica_groups=mesh['edge'=16,'node'=8] {'edge','node'}, dimensions={0} | all-to-all | bytes 2097152 | tf_op jit(solution)/shard_map/all_to_all | solution.py:347
  92.8 0.0 copy-done.1
  92.8 0.0 copy-done.3
  92.8 0.0 copy-done.5
  92.8 0.0 copy-done.6
  92.8 3.9 %lift.1 = f32[64,1024]{1,0:T(8,128)} custom-call(f32[2048,128]{1,0:T(8,128)S(1)} %bitcast.9, s32[1,1024]{1,0:T(1,128)S(1)} %get-tuple-element.14.slot_ref, f32[64,1024]{1,0:T(8,128)S(1)} %copy-done.5, f32[3,64,1024]{2,1,0:T(8,128)S(1)} %copy-done.1, f32[64,1024]{1,0:T(8,128)S(1)} %copy-done.6, s32[2,64,1024]{2,1,0:T(8,128)S(1)} %copy-done.3), custom_call_target="tpu_custom_call" | custom-call | tf_op jit(solution)/shard_map/lift/pallas_call | solution.py:330
  (5 shorter events, 0.0 us)
Async XLA Ops:
  0.0 1.1 %copy-start = (f32[3,64,1024]{2,1,0:T(8,128)S(1)}, f32[3,64,1024]{2,1,0:T(8,128)}, u32[]{:S(2)}) copy-start(f32[3,64,1024]{2,1,0:T(8,128)} %tan_ref.3) | copy-start | bytes 2359300
  1.1 1.0 %copy-start.2 = (s32[2,64,1024]{2,1,0:T(8,128)S(1)}, s32[2,64,1024]{2,1,0:T(8,128)}, u32[]{:S(2)}) copy-start(s32[2,64,1024]{2,1,0:T(8,128)} %ends_ref.3) | copy-start | bytes 1572868
  2.2 0.9 copy-start.4
  3.1 0.7 copy-start.7
  3.8 0.7 copy-start.8
  44.7 4.0 %copy-start.9 = (f32[4,32,256]{2,1,0:T(8,128)S(1)}, f32[4,32,256]{2,1,0:T(8,128)}, u32[]{:S(2)}) copy-start(f32[4,32,256]{2,1,0:T(8,128)} %param.13) | copy-start | bytes 393220
  47.6 9.0 %collective-permute-start = (f32[128,768]{1,0:T(8,128)S(1)}, f32[128,768]{1,0:T(8,128)S(1)}, u32[]{:S(2)}, u32[]{:S(2)}) collective-permute-start(f32[128,768]{1,0:T(8,128)S(1)} %get-tuple-element.12), channel_id=1, source_target_pairs={{0,1},{1,2},{2,3},{3,4},{4,5},{5,6},{6,7},{7,14},{14,15},{15,12},{... | collective-permute-start | bytes 1179656 | tf_op jit(solution)/shard_map/ppermute | solution.py:362
  48.7 7.9 %collective-permute-start.1 = (f32[128,768]{1,0:T(8,128)S(1)}, f32[128,768]{1,0:T(8,128)S(1)}, u32[]{:S(2)}, u32[]{:S(2)}) collective-permute-start(f32[128,768]{1,0:T(8,128)S(1)} %get-tuple-element.13), channel_id=1, source_target_pairs={{1,0},{2,1},{3,2},{4,3},{5,4},{6,5},{7,6},{14,7},{15,14},{12,15},{... | collective-permute-start | bytes 1179656 | tf_op jit(solution)/shard_map/ppermute | solution.py:363
  48.7 7.9 %collective-permute-start.2 = (f32[4,32,256]{2,1,0:T(8,128)S(1)}, f32[4,32,256]{2,1,0:T(8,128)S(1)}, u32[]{:S(2)}, u32[]{:S(2)}) collective-permute-start(f32[4,32,256]{2,1,0:T(8,128)S(1)} %copy-done.9), channel_id=1, source_target_pairs={{0,0},{1,1},{2,2},{3,3},{4,4},{5,5},{6,6},{7,7},{8,14},{9,15},{10,... | collective-permute-start | bytes 393224 | tf_op jit(solution)/shard_map/ppermute | solution.py:354
  49.4 7.2 %collective-permute-start.4 = (f32[2,32,256]{2,1,0:T(8,128)S(1)}, f32[2,32,256]{2,1,0:T(8,128)S(1)}, u32[]{:S(2)}, u32[]{:S(2)}) collective-permute-start(f32[2,32,256]{2,1,0:T(8,128)S(1)} %get-tuple-element.15), channel_id=1, source_target_pairs={{1,0},{2,1},{3,2},{4,3},{5,4},{6,5},{7,6},{8,7},{9,14},{10,15},{11... | collective-permute-start | bytes 196616 | tf_op jit(solution)/shard_map/ppermute | solution.py:356
  52.2 4.4 %collective-permute-start.3 = (f32[2,32,256]{2,1,0:T(8,128)S(1)}, f32[2,32,256]{2,1,0:T(8,128)S(1)}, u32[]{:S(2)}, u32[]{:S(2)}) collective-permute-start(f32[2,32,256]{2,1,0:T(8,128)S(1)} %get-tuple-element.16), channel_id=1, source_target_pairs={{0,1},{1,2},{2,3},{3,4},{4,5},{5,6},{6,7},{7,14},{8,15},{9,12},{10... | collective-permute-start | bytes 196616 | tf_op jit(solution)/shard_map/ppermute | solution.py:355
  62.2 30.6 %copy-start.1 = (f32[3,64,1024]{2,1,0:T(8,128)S(1)}, f32[3,64,1024]{2,1,0:T(8,128)}, u32[]{:S(2)}) copy-start(f32[3,64,1024]{2,1,0:T(8,128)} %tan_ref.3) | copy-start | bytes 2359300
  62.2 30.5 %copy-start.3 = (s32[2,64,1024]{2,1,0:T(8,128)S(1)}, s32[2,64,1024]{2,1,0:T(8,128)}, u32[]{:S(2)}) copy-start(s32[2,64,1024]{2,1,0:T(8,128)} %ends_ref.3) | copy-start | bytes 1572868
  62.2 30.5 %copy-start.5 = (f32[64,1024]{1,0:T(8,128)S(1)}, f32[64,1024]{1,0:T(8,128)}, u32[]{:S(2)}) copy-start(f32[64,1024]{1,0:T(8,128)} %res_ref.3) | copy-start | bytes 786436
  62.3 30.5 %copy-start.6 = (f32[64,1024]{1,0:T(8,128)S(1)}, f32[64,1024]{1,0:T(8,128)}, u32[]{:S(2)}) copy-start(f32[64,1024]{1,0:T(8,128)} %jac_ref.1) | copy-start | bytes 786436

commit v2 on v1

v2 whole, which is shorter than its diff:
```python
import jax
import jax.numpy as jnp
from jax import lax
from jax.experimental import pallas as pl
from jax.experimental.pallas import tpu as pltpu
from jax.sharding import PartitionSpec as P

F32 = jnp.float32
BF16 = jnp.bfloat16
I32 = jnp.int32

EDGES = 64
NODES = 32
ROW = 4 * NODES
BLOCKS = 1024
CAP = 16
DEVICES = 128
SLOTS = DEVICES * CAP
SLICE = 256
HALO = 3 * SLICE
LABEL = 3 * NODES
RING = ("edge", "node")
VMEM_LIMIT = 24 * 1024 * 1024
FIRST_LIMIT = 60 * 1024 * 1024
MESSAGE = ROW + 24

mass_scale = (1.0, 1.0, 1.0, 0.5)


def chebyshev_numbers(scale):
    upper = 12.0 + 8.0 * scale
    lower = upper / 8.0
    centre = (upper + lower) / 2.0
    radius = (upper - lower) / 2.0
    ratio = centre / radius
    first = 1.0 / ratio
    second = 1.0 / (2.0 * ratio - first)
    return (centre, second * first, 2.0 * second / radius)


def place(slab):
    return slab ^ (24 * ((slab >> 5) & 1)) ^ (6 * ((slab >> 3) & 1))


def split(value):
    high = value.astype(BF16)
    return high, (value - high.astype(F32)).astype(BF16)


def one_hot(mask):
    return jnp.where(mask, 1.0, 0.0).astype(BF16)


def iota(shape, dim):
    return lax.broadcasted_iota(I32, shape, dim)


def dot(left, right, dims):
    return lax.dot_general(left, right, (dims, ((), ())), preferred_element_type=F32)


def terms_kernel(
    target_hbm, block_hbm, res_hbm, tan_hbm, ends_hbm, send_hbm, slot_hbm,
    target_scr, block_scr, res_scr, tan_scr, ends_scr, term_scr, acc_scr, row_scr, send_scr, slot_ref, label_scr, place_scr,
    place_sem, list_sem, in_sem, out_sem,
):
    groups = BLOCKS // 128

    def fetch(group):
        lanes = pl.ds(group * 128, 128)
        return [
            pltpu.make_async_copy(hbm.at[..., lanes], scr.at[..., lanes], in_sem.at[i, group])
            for i, (hbm, scr) in enumerate(((ends_hbm, ends_scr), (res_hbm, res_scr), (tan_hbm, tan_scr)))
        ]

    lists = [
        pltpu.make_async_copy(target_hbm, target_scr, list_sem.at[0]),
        pltpu.make_async_copy(block_hbm, block_scr, list_sem.at[1]),
    ]
    for copy in lists:
        copy.start()
    for group in range(groups):
        for copy in fetch(group):
            copy.start()
    send_scr[...] = jnp.zeros((SLOTS, ROW), F32)
    node = iota((NODES, 128), 0)

    def turn(group):
        lanes = pl.ds(pl.multiple_of(group * 128, 128), 128)
        acc_scr[group, LABEL : LABEL + 1, :] = label_scr[:, lanes]
        row_scr[lanes, :] = acc_scr[group].T

    def post(group, step):
        for inner in range(16):
            block = group * 128 + step * 16 + inner
            send_scr[pl.ds(place_scr[0, block], 1), :] = row_scr[pl.ds(block, 1), :]

    def edge_step(step, lanes, sums):
        sums = list(sums)
        for inner in range(8):
            row = slice(inner, inner + 1)
            head = ends_scr[1, step, row, lanes] == node
            tail = ends_scr[0, step, row, lanes] == node
            either = head | tail
            value = res_scr[step, row, lanes]
            for channel in range(3):
                term = term_scr[channel, step, row, :]
                sums[channel] = sums[channel] + jnp.where(either, term, 0.0)
            sums[3] = sums[3] + jnp.where(head, value, jnp.where(tail, -value, 0.0))
        return tuple(sums)

    def lanes_step(group, turned, posted):
        lanes = pl.ds(pl.multiple_of(group * 128, 128), 128)
        for i, (hbm, scr) in enumerate(((ends_hbm, ends_scr), (res_hbm, res_scr), (tan_hbm, tan_scr))):
            pltpu.make_async_copy(hbm.at[..., lanes], scr.at[..., lanes], in_sem.at[i, group]).wait()
        term_scr[...] = 0.5 * tan_scr[:, :, :, lanes] * res_scr[:, :, lanes][None]
        if turned:
            turn(group - 1)
        if posted:
            post(group - 2, 0)
        sums = edge_step(0, lanes, (jnp.zeros((NODES, 128), F32),) * 4)

        def tile_step(step, sums):
            if posted:
                post(group - 2, step)
            return edge_step(step, lanes, sums)

        sums = lax.fori_loop(1, EDGES // 8, tile_step, sums)
        for channel in range(3):
            acc_scr[group, channel * NODES : (channel + 1) * NODES, :] = sums[channel]
        acc_scr[group, LABEL:, :] = sums[3]

    lanes_step(0, False, False)
    for copy in lists:
        copy.wait()

    holder = place(target_scr[...])
    device = iota((DEVICES, 128), 0)
    before = one_hot(iota((128, 128), 0) < iota((128, 128), 1))
    seen = jnp.zeros((DEVICES, 1), F32)
    for group in range(groups):
        lanes = slice(group * 128, (group + 1) * 128)
        same = holder[:, lanes] == device
        hot = jnp.where(same, 1.0, 0.0)
        count = dot(hot.astype(BF16), before, ((1,), (0,))) + seen
        rank = jnp.sum(jnp.where(same, count, 0.0), axis=0, keepdims=True)
        slot_ref[:, lanes] = holder[:, lanes] * CAP + rank.astype(I32)
        seen = seen + jnp.sum(hot, axis=1, keepdims=True)
    to_scalar = pltpu.make_async_copy(slot_ref, place_scr, place_sem.at[0])
    to_scalar.start()
    to_lift = pltpu.make_async_copy(slot_ref, slot_hbm, place_sem.at[1])
    to_lift.start()

    number = block_scr[...]
    label = (number & ~255) + (number & 7) * 32 + ((number >> 3) & 31)
    label = (label + 1).astype(F32)
    label_scr[...] = label

    lanes_step(1, True, False)
    to_scalar.wait()

    def group_step(group, _):
        lanes_step(group, True, True)
        return 0

    lax.fori_loop(2, groups, group_step, 0)
    turn(groups - 1)
    for group in (groups - 2, groups - 1):
        for step in range(8):
            post(group, step)
    parts = 8
    out = []
    for part in range(parts):
        rows = pl.ds(part * (SLOTS // parts), SLOTS // parts)
        out.append(pltpu.make_async_copy(send_scr.at[rows, :], send_hbm.at[rows, :], out_sem.at[part]))
    for copy in out:
        copy.start()
    for copy in out:
        copy.wait()
    to_lift.wait()


def edge_terms(residual, tangent, ends, target, node_block):
    tiles = EDGES // 8
    hbm = pl.BlockSpec(memory_space=pltpu.HBM)
    return pl.pallas_call(
        terms_kernel,
        out_shape=(
            jax.ShapeDtypeStruct((SLOTS, ROW), F32),
            jax.ShapeDtypeStruct((1, BLOCKS), I32),
        ),
        in_specs=[hbm] * 5,
        out_specs=[hbm, hbm],
        scratch_shapes=[
            pltpu.VMEM((1, BLOCKS), I32),
            pltpu.VMEM((1, BLOCKS), I32),
            pltpu.VMEM((tiles, 8, BLOCKS), F32),
            pltpu.VMEM((3, tiles, 8, BLOCKS), F32),
            pltpu.VMEM((2, tiles, 8, BLOCKS), I32),
            pltpu.VMEM((3, tiles, 8, 128), F32),
            pltpu.VMEM((BLOCKS // 128, ROW, 128), F32),
            pltpu.VMEM((BLOCKS, ROW), F32),
            pltpu.VMEM((SLOTS, ROW), F32),
            pltpu.VMEM((1, BLOCKS), I32),
            pltpu.VMEM((1, BLOCKS), F32),
            pltpu.SMEM((1, BLOCKS), I32),
            pltpu.SemaphoreType.DMA((2,)),
            pltpu.SemaphoreType.DMA((2,)),
            pltpu.SemaphoreType.DMA((3, BLOCKS // 128)),
            pltpu.SemaphoreType.DMA((8,)),
        ],
        compiler_params=pltpu.CompilerParams(vmem_limit_bytes=FIRST_LIMIT),
        cost_estimate=pl.CostEstimate(flops=50_000_000, bytes_accessed=20_000_000, transcendentals=0),
        name="edge_terms",
    )(
        target,
        node_block,
        residual.reshape(tiles, 8, BLOCKS),
        tangent.reshape(3, tiles, 8, BLOCKS),
        ends.reshape(2, tiles, 8, BLOCKS),
    )


def sums_kernel(got_ref, sigma_ref, own_ref, before_ref, after_ref, from_ref, sig_ref, rows_scr, hot_scr):
    for step in range(SLOTS // 128):
        part = slice(step * 128, (step + 1) * 128)
        turned = got_ref[part, :].T
        high, low = split(turned)
        rows_scr[0:ROW, part] = high
        rows_scr[ROW:, part] = low
        label = turned[LABEL : LABEL + 1, :].astype(I32)
        from_ref[step : step + 1, :] = jnp.maximum(label - 1, 0)
        column = got_ref[part, LABEL : LABEL + 1].astype(I32)
        hot_scr[part, :] = one_hot(column == iota((128, BLOCKS), 1) + 1)

    for step in range(BLOCKS // 256):
        lanes = slice(step * 256, (step + 1) * 256)
        both = dot(rows_scr[...], hot_scr[:, lanes], ((1,), (0,)))
        sums = both[:ROW] + both[ROW:]
        scalar = sums[LABEL:]
        first = iota((NODES, 256), 0) == 0
        rest = -jnp.sum(jnp.where(first, 0.0, scalar), axis=0, keepdims=True)
        own_ref[0:LABEL, lanes] = sums[:LABEL]
        own_ref[LABEL:, lanes] = jnp.where(first, rest, scalar)
    before_ref[0:ROW, :] = own_ref[:, 0:HALO]
    after_ref[0:ROW, :] = own_ref[:, BLOCKS - HALO :]

    for s in range(4):
        turned = sigma_ref[s].T
        for block in range(8):
            at = s * SLICE + block * 32
            sig_ref[:, at : at + 32] = turned[block * 32 : (block + 1) * 32, :]
    for ref, first in ((before_ref, 0), (after_ref, 2)):
        ref[ROW:, 0 : 2 * SLICE] = sig_ref[0:24, first * SLICE : (first + 2) * SLICE]
        for s in range(2):
            ref[ROW + 8 * s : ROW + 8 * s + 8, 2 * SLICE :] = sig_ref[24:, (first + s) * SLICE : (first + s + 1) * SLICE]
        ref[ROW + 16 :, 2 * SLICE :] = jnp.zeros((8, SLICE), F32)


def block_sums(got, sigma):
    vmem = pl.BlockSpec(memory_space=pltpu.VMEM)
    return pl.pallas_call(
        sums_kernel,
        out_shape=(
            jax.ShapeDtypeStruct((ROW, BLOCKS), F32),
            jax.ShapeDtypeStruct((MESSAGE, HALO), F32),
            jax.ShapeDtypeStruct((MESSAGE, HALO), F32),
            jax.ShapeDtypeStruct((SLOTS // 128, 128), I32),
            jax.ShapeDtypeStruct((NODES, BLOCKS), F32),
        ),
        in_specs=[vmem] * 2,
        out_specs=[vmem] * 5,
        scratch_shapes=[
            pltpu.VMEM((2 * ROW, SLOTS), BF16),
            pltpu.VMEM((SLOTS, BLOCKS), BF16),
        ],
        compiler_params=pltpu.CompilerParams(vmem_limit_bytes=VMEM_LIMIT),
        cost_estimate=pl.CostEstimate(flops=1_100_000_000, bytes_accessed=5_000_000, transcendentals=0),
        name="block_sums",
    )(got, sigma)


def sweeps_kernel(
    own_ref, prev_ref, next_ref, sig_ref, from_ref, back_ref,
    diag_scr, d_scr, y_scr, p_scr, keep_scr, sol_scr, row_scr,
):
    tiles = NODES // 8
    lane = iota((8, 128), 1)
    row = iota((8, 128), 0)
    low, high = (lane & 31) > 0, (lane & 31) < 31
    bottom, top = row == 0, row == 7

    def put(scr, s, half, tile, value):
        scr[s + 3, half, tile * 8 : tile * 8 + 8, :] = value

    def get(scr, s, half, tile):
        return scr[s + 3, half, tile * 8 : tile * 8 + 8, :]

    def beside(scr, s):
        here = [[get(scr, s, half, tile) for tile in range(tiles)] for half in range(2)]
        up = [[pltpu.roll(value, 1, 0) for value in part] for part in here]
        down = [[pltpu.roll(value, 7, 0) for value in part] for part in here]
        first = [pltpu.roll(part[-1], 32, 1) for part in up]
        last = [pltpu.roll(part[0], 96, 1) for part in down]
        first = [jnp.where(lane < 32, 0.0, first[0]), jnp.where(lane < 32, first[0], first[1])]
        last = [jnp.where(lane < 96, last[0], last[1]), jnp.where(lane < 96, last[1], 0.0)]
        sums = []
        for half in range(2):
            sums.append([])
            for tile in range(tiles):
                below = up[half][tile - 1] if tile else first[half]
                above = down[half][tile + 1] if tile < tiles - 1 else last[half]
                axial = jnp.where(bottom, below, up[half][tile]) + jnp.where(top, above, down[half][tile])
                value = here[half][tile]
                inner = jnp.where(low, pltpu.roll(value, 1, 1), 0.0)
                outer = jnp.where(high, pltpu.roll(value, 127, 1), 0.0)
                sums[half].append((axial + inner) + outer)
        return sums

    def apply(scr, s, kind):
        near = beside(scr, s)
        for half in range(2):
            for tile in range(tiles):
                here = get(scr, s, half, tile)
                beyond = get(scr, s - 1, half, tile) + get(scr, s + 1, half, tile)
                diag = diag_scr[kind, s + 2, half, tile * 8 : tile * 8 + 8, :]
                yield half, tile, here, diag * here - (beyond + near[half][tile])

    def keep_diag(s, half, rows, sig):
        for i, mass in enumerate((mass_scale[0], mass_scale[3])):
            diag_scr[i, s + 2, half, rows, :] = 6.0 + mass * sig

    every, upper, lower = slice(0, NODES), slice(0, 24), slice(24, NODES)
    for half in range(2):
        for s in range(4):
            keep_diag(s, half, every, sig_ref[:, s * SLICE + half * 128 : s * SLICE + half * 128 + 128])
        for ref, first in ((prev_ref, -2), (next_ref, 4)):
            for s in range(2):
                at = s * SLICE + half * 128
                keep_diag(first + s, half, upper, ref[ROW:, at : at + 128])
                at = 2 * SLICE + half * 128
                keep_diag(first + s, half, lower, ref[ROW + 8 * s : ROW + 8 * s + 8, at : at + 128])

    def channel_step(channel, _):
        scalar = channel == 3
        vector_numbers = chebyshev_numbers(mass_scale[0])
        scalar_numbers = chebyshev_numbers(mass_scale[3])
        _, one, two = [
            jnp.where(scalar, b, a).astype(F32) for a, b in zip(vector_numbers, scalar_numbers)
        ]
        invert = jnp.where(scalar, 1.0 / scalar_numbers[0], 1.0 / vector_numbers[0]).astype(F32)
        kind = jnp.where(scalar, 1, 0)
        base = channel * NODES

        def rows(tile):
            return pl.ds(pl.multiple_of(base + tile * 8, 8), 8)

        def source(s, half, tile):
            if s < 0:
                ref, s = prev_ref, s + 3
            elif s > 3:
                ref, s = next_ref, s - 4
            else:
                ref = own_ref
            return ref[rows(tile), s * SLICE + half * 128 : s * SLICE + half * 128 + 128]

        for s in range(-3, 7):
            for half in range(2):
                for tile in range(tiles):
                    put(d_scr, s, half, tile, source(s, half, tile) * invert)
        for s in range(-2, 6):
            for half, tile, here, applied in apply(d_scr, s, kind):
                rest = source(s, half, tile) - applied
                put(y_scr, s, half, tile, here + (one * here + two * rest))
        for s in range(-1, 5):
            for half, tile, here, applied in apply(y_scr, s, kind):
                rest = source(s, half, tile) - applied
                put(p_scr, s, half, tile, rest * invert)
                if 0 <= s < 4:
                    keep_scr[s, half, tile * 8 : tile * 8 + 8, :] = rest
        for s in range(4):
            for half, tile, here, applied in apply(p_scr, s, kind):
                rest = keep_scr[s, half, tile * 8 : tile * 8 + 8, :] - applied
                at = s * SLICE + half * 128
                value = (get(y_scr, s, half, tile) + here) + (one * here + two * rest)
                sol_scr[rows(tile), at : at + 128] = value
        return 0

    lax.fori_loop(0, 4, channel_step, 0)
    for group in range(BLOCKS // 128):
        part = slice(group * 128, (group + 1) * 128)
        row_scr[part, :] = sol_scr[:, part].T
    for slot in range(SLOTS):
        back_ref[slot : slot + 1, :] = row_scr[pl.ds(from_ref[slot // 128, slot % 128], 1), :]


def sweeps(own, prev_part, next_part, sig, labels):
    vmem = pl.BlockSpec(memory_space=pltpu.VMEM)
    field = pltpu.VMEM((10, 2, NODES, 128), F32)
    return pl.pallas_call(
        sweeps_kernel,
        out_shape=jax.ShapeDtypeStruct((SLOTS, ROW), F32),
        in_specs=[vmem, vmem, vmem, vmem, pl.BlockSpec(memory_space=pltpu.SMEM)],
        out_specs=vmem,
        scratch_shapes=[
            pltpu.VMEM((2, 8, 2, NODES, 128), F32),
            field,
            field,
            field,
            pltpu.VMEM((4, 2, NODES, 128), F32),
            pltpu.VMEM((ROW, BLOCKS), F32),
            pltpu.VMEM((BLOCKS, ROW), F32),
        ],
        compiler_params=pltpu.CompilerParams(vmem_limit_bytes=VMEM_LIMIT),
        name="sweeps",
    )(own, prev_part, next_part, sig, labels)


def lift_kernel(got_ref, slot_ref, res_ref, tan_ref, jac_ref, ends_ref, out_hbm, row_scr, y_scr, out_ref, out_sem):
    def take(group, step):
        for inner in range(16):
            block = group * 128 + step * 16 + inner
            row_scr[block : block + 1, :] = got_ref[pl.ds(slot_ref[0, block], 1), :]

    def turn(group):
        y_scr[group] = row_scr[group * 128 : (group + 1) * 128, :].T

    groups = BLOCKS // 128
    for step in range(8):
        take(0, step)
    turn(0)
    for group in range(groups):
        lanes = slice(group * 128, (group + 1) * 128)

        def pick(channel, low, quarter):
            parts = [
                jnp.take_along_axis(y_scr[group, channel * NODES + 8 * k : channel * NODES + 8 * k + 8, :], low, axis=0)
                for k in range(4)
            ]
            return jnp.where(
                quarter < 2,
                jnp.where(quarter == 0, parts[0], parts[1]),
                jnp.where(quarter == 2, parts[2], parts[3]),
            )

        for step in range(EDGES // 8):
            if group + 1 < groups:
                take(group + 1, step)
            edges = slice(step * 8, (step + 1) * 8)
            tail = ends_ref[0, edges, lanes]
            head = ends_ref[1, edges, lanes]
            tail_at = (tail & 7, tail >> 3)
            head_at = (head & 7, head >> 3)
            total = pick(3, *head_at) - pick(3, *tail_at)
            for channel in range(3):
                pair = pick(channel, *head_at) + pick(channel, *tail_at)
                total = total + 0.5 * tan_ref[channel, edges, lanes] * pair
            out_ref[edges, lanes] = jac_ref[edges, lanes] * res_ref[edges, lanes] + total
        if group + 1 < groups:
            turn(group + 1)
        pltpu.make_async_copy(out_ref.at[:, lanes], out_hbm.at[:, lanes], out_sem.at[group]).start()
    for group in range(groups):
        lanes = slice(group * 128, (group + 1) * 128)
        pltpu.make_async_copy(out_ref.at[:, lanes], out_hbm.at[:, lanes], out_sem.at[group]).wait()


def lift(got, slots, residual, tangent, jacobi, ends):
    vmem = pl.BlockSpec(memory_space=pltpu.VMEM)
    return pl.pallas_call(
        lift_kernel,
        out_shape=jax.ShapeDtypeStruct((EDGES, BLOCKS), F32),
        in_specs=[vmem, pl.BlockSpec(memory_space=pltpu.SMEM), vmem, vmem, vmem, vmem],
        out_specs=pl.BlockSpec(memory_space=pltpu.HBM),
        scratch_shapes=[
            pltpu.VMEM((BLOCKS, ROW), F32),
            pltpu.VMEM((BLOCKS // 128, ROW, 128), F32),
            pltpu.VMEM((EDGES, BLOCKS), F32),
            pltpu.SemaphoreType.DMA((BLOCKS // 128,)),
        ],
        compiler_params=pltpu.CompilerParams(vmem_limit_bytes=VMEM_LIMIT),
        name="lift",
    )(got, slots, residual, tangent, jacobi, ends)


def exchange(rows):
    parts = rows.reshape(DEVICES, CAP, ROW)
    return lax.all_to_all(parts, RING, split_axis=0, concat_axis=0, tiled=True).reshape(SLOTS, ROW)


def per_device(residual, tangent, jacobi, ends, target, node_block, sigma):
    slabs = range(DEVICES)
    forward = [(place(s), place((s + 1) % DEVICES)) for s in slabs]
    backward = [(place((s + 1) % DEVICES), place(s)) for s in slabs]
    sig_own = lax.ppermute(sigma, RING, [(s, place(s)) for s in slabs])
    send, slots = edge_terms(
        residual, tangent, ends, target.reshape(1, BLOCKS), node_block.reshape(1, BLOCKS)
    )
    send, sig_own = lax.optimization_barrier((send, sig_own))
    got = exchange(send)
    own, to_prev, to_next, labels, sig = block_sums(got, sig_own)
    prev_part = lax.ppermute(to_next, RING, forward)
    next_part = lax.ppermute(to_prev, RING, backward)
    back = sweeps(own, prev_part, next_part, sig, labels)
    mine = exchange(back)
    return lift(mine, slots, residual, tangent, jacobi, ends)


def solution(mesh):
    in_specs = (
        P(None, RING),
        P(None, None, RING),
        P(None, RING),
        P(None, None, RING),
        P(RING, None),
        P(RING),
        P(RING, None, None),
    )
    return jax.shard_map(
        per_device, mesh=mesh, in_specs=in_specs, out_specs=P(None, RING), check_vma=False
    )
```

time: 97 us -> 82.9 us (0.85)
  Pallas kernels: 21.9 us -> 16.1 us
  blocking collectives: 61.2 us -> 55.5 us
  local copies, waits for them, and re-layouts: 4.54 us -> 0.03 us
  waiting for transfers between devices: 4.38 us -> 8.29 us
  starting transfers between devices: 4.63 us -> 2.68 us
    all_to_all x2, blocking collectives: 61.2 us -> 55.5 us  [exchange(): lax.all_to_all(parts, RING, split_axis=0, concat_axis=0, tiled=True)]
    ppermute x1, waiting for transfers between devices: 0.01 us -> 5.51 us  [per_device(): prev_part = lax.ppermute(to_next, RING, forward)]
    unnamed x20 -> x10, local copies, waits for them, and re-layouts: 4.52 us -> 0.03 us
    ppermute x2 -> x0, waiting for transfers between devices: 4.38 us -> none  [the longest x1 4.37 us: per_device(): lax.ppermute(sigma[:2], RING, [((s + 1) % DEVICES, place(s)) for s in sla...]
    ppermute x2 -> x0, starting transfers between devices: 2.84 us -> none  [the longest x1 2.84 us: per_device(): lax.ppermute(sigma[:2], RING, [((s + 1) % DEVICES, place(s)) for s in sla...]
    ppermute x1, waiting for transfers between devices: 0.01 us -> 2.77 us  [per_device(): next_part = lax.ppermute(to_prev, RING, backward)]
    pallas_call x1, Pallas kernels: 9.55 us -> 7.03 us  [edge_terms(): pl.pallas_call(terms_kernel, out_shape=(jax.ShapeDtypeStruct((SLOTS, ROW)...]
    pallas_call x1, Pallas kernels: 2.85 us -> 1.62 us  [block_sums(): pl.pallas_call(sums_kernel, out_shape=(jax.ShapeDtypeStruct((ROW, BLOCKS)...]
  transfers between devices with their start and end apart: 5 -> 3, of which waited for: 1 -> 2; matrix products, arithmetic and copies ran while one was open for 0% -> 0% of each run, Pallas kernels for 0% -> 9%
where the time goes in v2:
time: 82.9 us; the launch traced here: 82.6 us
  blocking collectives  55.5 us (67%)
  Pallas kernels  16.1 us (19%)
  waiting for transfers between devices  8.29 us (10%)
  starting transfers between devices  2.68 us (3%)
    all_to_all x2, blocking collectives, exchange(): lax.all_to_all(parts, RING, split_axis=0, concat_axis=0, tiled=True)  55.5 us
    pallas_call x1, Pallas kernels, edge_terms(): pl.pallas_call(terms_kernel, out_shape=(jax.ShapeDtypeStruct((SLOTS, ROW)...  7.03 us
    ppermute x1, waiting for transfers between devices, per_device(): prev_part = lax.ppermute(to_next, RING, forward)  5.51 us
    pallas_call x1, Pallas kernels, sweeps(): pl.pallas_call(sweeps_kernel, out_shape=jax.ShapeDtypeStruct((SLOTS, ROW)...  4.71 us
    ppermute x1, waiting for transfers between devices, per_device(): next_part = lax.ppermute(to_prev, RING, backward)  2.77 us
    pallas_call x1, Pallas kernels, lift(): pl.pallas_call(lift_kernel, out_shape=jax.ShapeDtypeStruct((EDGES, BLOCKS...  2.71 us
  transfers between devices with their start and end apart: 3, of which 2 were waited for; matrix products, arithmetic and copies ran while one was open for 0% of the time, Pallas kernels for 9%

profile of v2, /device:TPU:1, one launch (start us, length us, event | category | flops | bytes accessed | tf_op | source)
XLA Modules:
  0.0 82.6 jit_solution(9444385341024705646)
XLA Ops:
  0.0 1.6 %collective-permute-start = (f32[4,32,256]{2,1,0:T(8,128)}, f32[4,32,256]{2,1,0:T(8,128)S(1)}, u32[]{:S(2)}, u32[]{:S(2)}) collective-permute-start(f32[4,32,256]{2,1,0:T(8,128)} %param.13), channel_id=1, source_target_pairs={{0,0},{1,1},{2,2},{3,3},{4,4},{5,5},{6,6},{7,7},{8,14},{9,15},{10,... | collective-permute-start | bytes 393224 | tf_op jit(solution)/shard_map/ppermute | solution.py:494
  1.6 7.0 %edge_terms.1 = (f32[2048,128]{1,0:T(8,128)}, s32[1,1024]{1,0:T(1,128)}) custom-call(s32[1,1024]{1,0:T(1,128)} %bitcast.16, s32[1,1024]{1,0:T(1,128)} %bitcast.17, f32[8,8,1024]{2,1,0:T(8,128)} %bitcast.14, f32[3,8,8,1024]{3,2,1,0:T(8,128)} %bitcast.11, s32[2,8,8,1024]{3,2,1,0:T(8,128)} %bitcast.12), custom_call_target="tpu_custom_call" | custom-call | flops 50000000 | bytes 20000000 | tf_op jit(solution)/shard_map/edge_terms/pallas_call | solution.py:186
  8.6 0.0 collective-permute-done.sigma_ref
  8.6 31.8 %all_to_all.10 = f32[128,16,128]{2,1,0:T(8,128)S(1)} all-to-all(f32[128,16,128]{2,1,0:T(8,128)} %bitcast.15), channel_id=1, replica_groups=mesh['edge'=16,'node'=8] {'edge','node'}, dimensions={0} | all-to-all | bytes 2097152 | tf_op jit(solution)/shard_map/all_to_all | solution.py:487
  40.4 1.6 %block_sums.1 = (f32[128,1024]{1,0:T(8,128)S(1)}, f32[152,768]{1,0:T(8,128)S(1)}, f32[152,768]{1,0:T(8,128)S(1)}, s32[16,128]{1,0:T(8,128)S(1)}, f32[32,1024]{1,0:T(8,128)S(1)}) custom-call(f32[2048,128]{1,0:T(8,128)S(1)} %bitcast.13, f32[4,32,256]{2,1,0:T(8,128)S(1)} %collective-permute-done.sigma_ref), custom_call_target="tpu_custom_call" | custom-call | flops 1100000000 | bytes 5000000 | tf_op jit(solution)/shard_map/block_sums/pallas_call | solution.py:262
  42.0 1.1 %collective-permute-start.1 = (f32[152,768]{1,0:T(8,128)S(1)}, f32[152,768]{1,0:T(8,128)S(1)}, u32[]{:S(2)}, u32[]{:S(2)}) collective-permute-start(f32[152,768]{1,0:T(8,128)S(1)} %get-tuple-element.18), channel_id=1, source_target_pairs={{0,1},{1,2},{2,3},{3,4},{4,5},{5,6},{6,7},{7,14},{14,15},{15,12},{... | collective-permute-start | bytes 1400840 | tf_op jit(solution)/shard_map/ppermute | solution.py:501
  43.1 0.0 collective-permute-start.2
  43.1 5.5 %collective-permute-done.1.prev_ref = f32[152,768]{1,0:T(8,128)S(1)} collective-permute-done((f32[152,768]{1,0:T(8,128)S(1)}, f32[152,768]{1,0:T(8,128)S(1)}, u32[]{:S(2)}, u32[]{:S(2)}) %collective-permute-start.1) | collective-permute-done | bytes 466976 | tf_op jit(solution)/shard_map/ppermute | solution.py:501
  48.6 2.8 %collective-permute-done.2.next_ref = f32[152,768]{1,0:T(8,128)S(1)} collective-permute-done((f32[152,768]{1,0:T(8,128)S(1)}, f32[152,768]{1,0:T(8,128)S(1)}, u32[]{:S(2)}, u32[]{:S(2)}) %collective-permute-start.2) | collective-permute-done | bytes 466976 | tf_op jit(solution)/shard_map/ppermute | solution.py:502
  51.4 4.7 %sweeps.1 = f32[2048,128]{1,0:T(8,128)S(1)} custom-call(f32[128,1024]{1,0:T(8,128)S(1)} %get-tuple-element.17.own_ref, f32[152,768]{1,0:T(8,128)S(1)} %collective-permute-done.1.prev_ref, f32[152,768]{1,0:T(8,128)S(1)} %collective-permute-done.2.next_ref, f32[32,1024]{1,0:T(8,128)S(1)} %get-tuple-element.20.sig_ref, s32[16,128]{1,0:T(8,128)S(1)} %get-tuple-element.21.from_ref), custom_call_target="tpu_custom_call" | custom-call | tf_op jit(solution)/shard_map/sweeps/pallas_call | solution.py:400
  56.1 0.0 copy-start
  56.1 0.0 copy-start.1
  56.1 0.0 copy-start.2
  56.2 0.0 copy-start.3
  56.2 0.0 copy-start.4
  56.2 23.7 %all_to_all.11 = f32[128,16,128]{2,1,0:T(8,128)S(1)} all-to-all(f32[128,16,128]{2,1,0:T(8,128)S(1)} %bitcast.9), channel_id=1, replica_groups=mesh['edge'=16,'node'=8] {'edge','node'}, dimensions={0} | all-to-all | bytes 2097152 | tf_op jit(solution)/shard_map/all_to_all | solution.py:487
  79.9 0.0 copy-done
  79.9 0.0 copy-done.1
  79.9 0.0 copy-done.2
  79.9 0.0 copy-done.3
  79.9 0.0 copy-done.4
  79.9 2.7 %lift.1 = f32[64,1024]{1,0:T(8,128)} custom-call(f32[2048,128]{1,0:T(8,128)S(1)} %bitcast.10, s32[1,1024]{1,0:T(1,128)S(1)} %copy-done.4, f32[64,1024]{1,0:T(8,128)S(1)} %copy-done.2, f32[3,64,1024]{2,1,0:T(8,128)S(1)} %copy-done, f32[64,1024]{1,0:T(8,128)S(1)} %copy-done.3, s32[2,64,1024]{2,1,0:T(8,128)S(1)} %copy-done.1), custom_call_target="tpu_custom_call" | custom-call | tf_op jit(solution)/shard_map/lift/pallas_call | solution.py:469
Async XLA Ops:
  0.0 8.6 %collective-permute-start = (f32[4,32,256]{2,1,0:T(8,128)}, f32[4,32,256]{2,1,0:T(8,128)S(1)}, u32[]{:S(2)}, u32[]{:S(2)}) collective-permute-start(f32[4,32,256]{2,1,0:T(8,128)} %param.13), channel_id=1, source_target_pairs={{0,0},{1,1},{2,2},{3,3},{4,4},{5,5},{6,6},{7,7},{8,14},{9,15},{10,... | collective-permute-start | bytes 393224 | tf_op jit(solution)/shard_map/ppermute | solution.py:494
  42.0 6.6 %collective-permute-start.1 = (f32[152,768]{1,0:T(8,128)S(1)}, f32[152,768]{1,0:T(8,128)S(1)}, u32[]{:S(2)}, u32[]{:S(2)}) collective-permute-start(f32[152,768]{1,0:T(8,128)S(1)} %get-tuple-element.18), channel_id=1, source_target_pairs={{0,1},{1,2},{2,3},{3,4},{4,5},{5,6},{6,7},{7,14},{14,15},{15,12},{... | collective-permute-start | bytes 1400840 | tf_op jit(solution)/shard_map/ppermute | solution.py:501
  43.1 8.3 %collective-permute-start.2 = (f32[152,768]{1,0:T(8,128)S(1)}, f32[152,768]{1,0:T(8,128)S(1)}, u32[]{:S(2)}, u32[]{:S(2)}) collective-permute-start(f32[152,768]{1,0:T(8,128)S(1)} %get-tuple-element.19), channel_id=1, source_target_pairs={{1,0},{2,1},{3,2},{4,3},{5,4},{6,5},{7,6},{14,7},{15,14},{12,15},{... | collective-permute-start | bytes 1400840 | tf_op jit(solution)/shard_map/ppermute | solution.py:502
  56.1 23.8 %copy-start = (f32[3,64,1024]{2,1,0:T(8,128)S(1)}, f32[3,64,1024]{2,1,0:T(8,128)}, u32[]{:S(2)}) copy-start(f32[3,64,1024]{2,1,0:T(8,128)} %tan_ref.1) | copy-start | bytes 2359300
  56.1 23.8 %copy-start.1 = (s32[2,64,1024]{2,1,0:T(8,128)S(1)}, s32[2,64,1024]{2,1,0:T(8,128)}, u32[]{:S(2)}) copy-start(s32[2,64,1024]{2,1,0:T(8,128)} %ends_ref.1) | copy-start | bytes 1572868
  56.1 23.7 %copy-start.2 = (f32[64,1024]{1,0:T(8,128)S(1)}, f32[64,1024]{1,0:T(8,128)}, u32[]{:S(2)}) copy-start(f32[64,1024]{1,0:T(8,128)} %res_ref.1) | copy-start | bytes 786436
  56.2 23.7 %copy-start.3 = (f32[64,1024]{1,0:T(8,128)S(1)}, f32[64,1024]{1,0:T(8,128)}, u32[]{:S(2)}) copy-start(f32[64,1024]{1,0:T(8,128)} %jac_ref.1) | copy-start | bytes 786436
  56.2 23.7 %copy-start.4 = (s32[1,1024]{1,0:T(1,128)S(1)}, s32[1,1024]{1,0:T(1,128)}, u32[]{:S(2)}) copy-start(s32[1,1024]{1,0:T(1,128)} %get-tuple-element.22.slot_ref) | copy-start | bytes 12292

commit v3 on v2

--- a/solution.py
+++ b/solution.py
@@ -42,6 +42,10 @@
     return slab ^ (24 * ((slab >> 5) & 1)) ^ (6 * ((slab >> 3) & 1))
 
 
+def odd_slab():
+    return lax.axis_index("node") & 1
+
+
 def split(value):
     high = value.astype(BF16)
     return high, (value - high.astype(F32)).astype(BF16)
@@ -66,10 +70,12 @@
 ):
     groups = BLOCKS // 128
 
-    def fetch(group):
-        lanes = pl.ds(group * 128, 128)
+    chunks = ((0, 128), (128, 128), (256, BLOCKS - 256))
+
+    def fetch(chunk):
+        lanes = pl.ds(*chunks[chunk])
         return [
-            pltpu.make_async_copy(hbm.at[..., lanes], scr.at[..., lanes], in_sem.at[i, group])
+            pltpu.make_async_copy(hbm.at[..., lanes], scr.at[..., lanes], in_sem.at[i, chunk])
             for i, (hbm, scr) in enumerate(((ends_hbm, ends_scr), (res_hbm, res_scr), (tan_hbm, tan_scr)))
         ]
 
@@ -77,11 +83,9 @@
         pltpu.make_async_copy(target_hbm, target_scr, list_sem.at[0]),
         pltpu.make_async_copy(block_hbm, block_scr, list_sem.at[1]),
     ]
-    for copy in lists:
+    fetched = [fetch(chunk) for chunk in range(3)]
+    for copy in fetched[0] + lists + fetched[1] + fetched[2]:
         copy.start()
-    for group in range(groups):
-        for copy in fetch(group):
-            copy.start()
     send_scr[...] = jnp.zeros((SLOTS, ROW), F32)
     node = iota((NODES, 128), 0)
 
@@ -111,8 +115,6 @@
 
     def lanes_step(group, turned, posted):
         lanes = pl.ds(pl.multiple_of(group * 128, 128), 128)
-        for i, (hbm, scr) in enumerate(((ends_hbm, ends_scr), (res_hbm, res_scr), (tan_hbm, tan_scr))):
-            pltpu.make_async_copy(hbm.at[..., lanes], scr.at[..., lanes], in_sem.at[i, group]).wait()
         term_scr[...] = 0.5 * tan_scr[:, :, :, lanes] * res_scr[:, :, lanes][None]
         if turned:
             turn(group - 1)
@@ -130,6 +132,8 @@
             acc_scr[group, channel * NODES : (channel + 1) * NODES, :] = sums[channel]
         acc_scr[group, LABEL:, :] = sums[3]
 
+    for copy in fetched[0]:
+        copy.wait()
     lanes_step(0, False, False)
     for copy in lists:
         copy.wait()
@@ -156,7 +160,11 @@
     label = (label + 1).astype(F32)
     label_scr[...] = label
 
+    for copy in fetched[1]:
+        copy.wait()
     lanes_step(1, True, False)
+    for copy in fetched[2]:
+        copy.wait()
     to_scalar.wait()
 
     def group_step(group, _):
@@ -206,7 +214,7 @@
             pltpu.SMEM((1, BLOCKS), I32),
             pltpu.SemaphoreType.DMA((2,)),
             pltpu.SemaphoreType.DMA((2,)),
-            pltpu.SemaphoreType.DMA((3, BLOCKS // 128)),
+            pltpu.SemaphoreType.DMA((3, 3)),
             pltpu.SemaphoreType.DMA((8,)),
         ],
         compiler_params=pltpu.CompilerParams(vmem_limit_bytes=FIRST_LIMIT),
@@ -221,7 +229,7 @@
     )
 
 
-def sums_kernel(got_ref, sigma_ref, own_ref, before_ref, after_ref, from_ref, sig_ref, rows_scr, hot_scr):
+def sums_kernel(got_ref, sigma_ref, own_ref, far_ref, near_ref, from_ref, sig_ref, rows_scr, hot_scr):
     for step in range(SLOTS // 128):
         part = slice(step * 128, (step + 1) * 128)
         turned = got_ref[part, :].T
@@ -242,18 +250,19 @@
         rest = -jnp.sum(jnp.where(first, 0.0, scalar), axis=0, keepdims=True)
         own_ref[0:LABEL, lanes] = sums[:LABEL]
         own_ref[LABEL:, lanes] = jnp.where(first, rest, scalar)
-    before_ref[0:ROW, :] = own_ref[:, 0:HALO]
-    after_ref[0:ROW, :] = own_ref[:, BLOCKS - HALO :]
-
     for s in range(4):
         turned = sigma_ref[s].T
         for block in range(8):
             at = s * SLICE + block * 32
             sig_ref[:, at : at + 32] = turned[block * 32 : (block + 1) * 32, :]
-    for ref, first in ((before_ref, 0), (after_ref, 2)):
-        ref[ROW:, 0 : 2 * SLICE] = sig_ref[0:24, first * SLICE : (first + 2) * SLICE]
+    odd = odd_slab()
+    for ref, after in ((far_ref, odd), (near_ref, 1 - odd)):
+        ref[0:ROW, :] = own_ref[:, pl.ds(pl.multiple_of(after * SLICE, SLICE), HALO)]
+        lanes = pl.ds(pl.multiple_of(after * (2 * SLICE), 2 * SLICE), 2 * SLICE)
+        ref[ROW:, 0 : 2 * SLICE] = sig_ref[0:24, lanes]
         for s in range(2):
-            ref[ROW + 8 * s : ROW + 8 * s + 8, 2 * SLICE :] = sig_ref[24:, (first + s) * SLICE : (first + s + 1) * SLICE]
+            lanes = pl.ds(pl.multiple_of((2 * after + s) * SLICE, SLICE), SLICE)
+            ref[ROW + 8 * s : ROW + 8 * s + 8, 2 * SLICE :] = sig_ref[24:, lanes]
         ref[ROW + 16 :, 2 * SLICE :] = jnp.zeros((8, SLICE), F32)
 
 
@@ -281,9 +290,17 @@
 
 
 def sweeps_kernel(
-    own_ref, prev_ref, next_ref, sig_ref, from_ref, back_ref,
-    diag_scr, d_scr, y_scr, p_scr, keep_scr, sol_scr, row_scr,
+    own_ref, far_ref, near_ref, sig_ref, from_ref, back_ref,
+    diag_scr, d_scr, y_scr, p_scr, keep_scr, sol_scr, row_scr, place_scr, place_sem,
 ):
+    to_scalar = pltpu.make_async_copy(from_ref, place_scr, place_sem)
+    to_scalar.start()
+    odd = odd_slab() == 1
+
+    def halo(behind, index):
+        far, near = far_ref[index], near_ref[index]
+        return jnp.where(odd, near, far) if behind else jnp.where(odd, far, near)
+
     tiles = NODES // 8
     lane = iota((8, 128), 1)
     row = iota((8, 128), 0)
@@ -334,12 +351,14 @@
     for half in range(2):
         for s in range(4):
             keep_diag(s, half, every, sig_ref[:, s * SLICE + half * 128 : s * SLICE + half * 128 + 128])
-        for ref, first in ((prev_ref, -2), (next_ref, 4)):
+        for behind, first in ((True, -2), (False, 4)):
             for s in range(2):
                 at = s * SLICE + half * 128
-                keep_diag(first + s, half, upper, ref[ROW:, at : at + 128])
+                sig = halo(behind, (slice(ROW, ROW + 24), slice(at, at + 128)))
+                keep_diag(first + s, half, upper, sig)
                 at = 2 * SLICE + half * 128
-                keep_diag(first + s, half, lower, ref[ROW + 8 * s : ROW + 8 * s + 8, at : at + 128])
+                sig = halo(behind, (slice(ROW + 8 * s, ROW + 8 * s + 8), slice(at, at + 128)))
+                keep_diag(first + s, half, lower, sig)
 
     def channel_step(channel, _):
         scalar = channel == 3
@@ -356,13 +375,11 @@
             return pl.ds(pl.multiple_of(base + tile * 8, 8), 8)
 
         def source(s, half, tile):
-            if s < 0:
-                ref, s = prev_ref, s + 3
-            elif s > 3:
-                ref, s = next_ref, s - 4
-            else:
-                ref = own_ref
-            return ref[rows(tile), s * SLICE + half * 128 : s * SLICE + half * 128 + 128]
+            behind, beyond = s < 0, s < 0 or s > 3
+            if beyond:
+                s = s + 3 if behind else s - 4
+            index = (rows(tile), slice(s * SLICE + half * 128, s * SLICE + half * 128 + 128))
+            return halo(behind, index) if beyond else own_ref[index]
 
         for s in range(-3, 7):
             for half in range(2):
@@ -390,17 +407,18 @@
     for group in range(BLOCKS // 128):
         part = slice(group * 128, (group + 1) * 128)
         row_scr[part, :] = sol_scr[:, part].T
+    to_scalar.wait()
     for slot in range(SLOTS):
-        back_ref[slot : slot + 1, :] = row_scr[pl.ds(from_ref[slot // 128, slot % 128], 1), :]
-
-
-def sweeps(own, prev_part, next_part, sig, labels):
+        back_ref[slot : slot + 1, :] = row_scr[pl.ds(place_scr[slot // 128, slot % 128], 1), :]
+
+
+def sweeps(own, far, near, sig, labels):
     vmem = pl.BlockSpec(memory_space=pltpu.VMEM)
     field = pltpu.VMEM((10, 2, NODES, 128), F32)
     return pl.pallas_call(
         sweeps_kernel,
         out_shape=jax.ShapeDtypeStruct((SLOTS, ROW), F32),
-        in_specs=[vmem, vmem, vmem, vmem, pl.BlockSpec(memory_space=pltpu.SMEM)],
+        in_specs=[vmem] * 5,
         out_specs=vmem,
         scratch_shapes=[
             pltpu.VMEM((2, 8, 2, NODES, 128), F32),
@@ -410,10 +428,12 @@
             pltpu.VMEM((4, 2, NODES, 128), F32),
             pltpu.VMEM((ROW, BLOCKS), F32),
             pltpu.VMEM((BLOCKS, ROW), F32),
+            pltpu.SMEM((SLOTS // 128, 128), I32),
+            pltpu.SemaphoreType.DMA,
         ],
         compiler_params=pltpu.CompilerParams(vmem_limit_bytes=VMEM_LIMIT),
         name="sweeps",
-    )(own, prev_part, next_part, sig, labels)
+    )(own, far, near, sig, labels)
 
 
 def lift_kernel(got_ref, slot_ref, res_ref, tan_ref, jac_ref, ends_ref, out_hbm, row_scr, y_scr, out_ref, out_sem):
@@ -489,18 +509,17 @@
 
 def per_device(residual, tangent, jacobi, ends, target, node_block, sigma):
     slabs = range(DEVICES)
-    forward = [(place(s), place((s + 1) % DEVICES)) for s in slabs]
-    backward = [(place((s + 1) % DEVICES), place(s)) for s in slabs]
+    between = [(place(s), place((s + 1 if s % 2 else s - 1) % DEVICES)) for s in slabs]
+    within = [(place(s), place(s ^ 1)) for s in slabs]
     sig_own = lax.ppermute(sigma, RING, [(s, place(s)) for s in slabs])
     send, slots = edge_terms(
         residual, tangent, ends, target.reshape(1, BLOCKS), node_block.reshape(1, BLOCKS)
     )
-    send, sig_own = lax.optimization_barrier((send, sig_own))
     got = exchange(send)
-    own, to_prev, to_next, labels, sig = block_sums(got, sig_own)
-    prev_part = lax.ppermute(to_next, RING, forward)
-    next_part = lax.ppermute(to_prev, RING, backward)
-    back = sweeps(own, prev_part, next_part, sig, labels)
+    own, far, near, labels, sig = block_sums(got, sig_own)
+    far = lax.ppermute(far, RING, between)
+    near = lax.ppermute(near, RING, within)
+    back = sweeps(own, far, near, sig, labels)
     mine = exchange(back)
     return lift(mine, slots, residual, tangent, jacobi, ends)
 

time: 82.9 us -> 78.5 us (0.947)
  blocking collectives: 55.5 us -> 24.1 us
  waiting for transfers between devices: 8.29 us -> 24 us
  starting transfers between devices: 2.68 us -> 15.3 us
  Pallas kernels: 16.1 us -> 14.6 us
    all_to_all x2 -> x1, blocking collectives: 55.5 us -> 24.1 us  [exchange(): lax.all_to_all(parts, RING, split_axis=0, concat_axis=0, tiled=True)]
    all_to_all x0 -> x1, waiting for transfers between devices: none -> 18.8 us  [exchange(): lax.all_to_all(parts, RING, split_axis=0, concat_axis=0, tiled=True)]
    all_to_all x0 -> x1, starting transfers between devices: none -> 11.5 us  [exchange(): lax.all_to_all(parts, RING, split_axis=0, concat_axis=0, tiled=True)]
    ppermute x2, waiting for transfers between devices: 8.28 us -> 5.2 us  [the longest x1 5.2 us: per_device(): far = lax.ppermute(far, RING, between)]
    ppermute x2, starting transfers between devices: 1.13 us -> 3.16 us  [the longest x1 2.16 us: per_device(): near = lax.ppermute(near, RING, within)]
    pallas_call x1, Pallas kernels: 4.71 us -> 3.39 us  [sweeps(): pl.pallas_call(sweeps_kernel, out_shape=jax.ShapeDtypeStruct((SLOTS, ROW)...]
    ppermute x1, starting transfers between devices: 1.55 us -> 0.67 us  [per_device(): sig_own = lax.ppermute(sigma, RING, [(s, place(s)) for s in slabs])]
  transfers between devices with their start and end apart: 3 -> 4, of which waited for: 2 -> 2; matrix products, arithmetic and copies ran while one was open for 0% -> 0% of each run, Pallas kernels for 9% -> 0%
where the time goes in v3:
time: 78.5 us; the launch traced here: 78.2 us
  blocking collectives  24.1 us (31%)
  waiting for transfers between devices  24 us (31%)
  starting transfers between devices  15.3 us (19%)
  Pallas kernels  14.6 us (19%)
    all_to_all x1, blocking collectives, exchange(): lax.all_to_all(parts, RING, split_axis=0, concat_axis=0, tiled=True)  24.1 us
    all_to_all x1, waiting for transfers between devices, exchange(): lax.all_to_all(parts, RING, split_axis=0, concat_axis=0, tiled=True)  18.8 us
    all_to_all x1, starting transfers between devices, exchange(): lax.all_to_all(parts, RING, split_axis=0, concat_axis=0, tiled=True)  11.5 us
    pallas_call x1, Pallas kernels, edge_terms(): pl.pallas_call(terms_kernel, out_shape=(jax.ShapeDtypeStruct((SLOTS, ROW)...  6.83 us
    ppermute x1, waiting for transfers between devices, per_device(): far = lax.ppermute(far, RING, between)  5.2 us
    pallas_call x1, Pallas kernels, sweeps(): pl.pallas_call(sweeps_kernel, out_shape=jax.ShapeDtypeStruct((SLOTS, ROW)...  3.39 us
    pallas_call x1, Pallas kernels, lift(): pl.pallas_call(lift_kernel, out_shape=jax.ShapeDtypeStruct((EDGES, BLOCKS...  2.7 us
    ppermute x1, starting transfers between devices, per_device(): near = lax.ppermute(near, RING, within)  2.16 us
  transfers between devices with their start and end apart: 4, of which 2 were waited for; matrix products, arithmetic and copies ran while one was open for 0% of the time, Pallas kernels for 0%

profile of v3, /device:TPU:1, one launch (start us, length us, event | category | flops | bytes accessed | tf_op | source)
XLA Modules:
  0.0 78.2 jit_solution(11615566585177390242)
XLA Ops:
  0.0 6.8 %edge_terms.1 = (f32[2048,128]{1,0:T(8,128)}, s32[1,1024]{1,0:T(1,128)}) custom-call(s32[1,1024]{1,0:T(1,128)} %bitcast.16, s32[1,1024]{1,0:T(1,128)} %bitcast.17, f32[8,8,1024]{2,1,0:T(8,128)} %bitcast.14, f32[3,8,8,1024]{3,2,1,0:T(8,128)} %bitcast.11, s32[2,8,8,1024]{3,2,1,0:T(8,128)} %bitcast.12), custom_call_target="tpu_custom_call" | custom-call | flops 50000000 | bytes 20000000 | tf_op jit(solution)/shard_map/edge_terms/pallas_call | solution.py:194
  6.8 0.0 copy-start.5
  6.9 11.5 %all-to-all-start = ((f32[128,16,128]{2,1,0:T(8,128)}), f32[128,16,128]{2,1,0:T(8,128)S(1)}, u32[]{:S(2)}, u32[]{:S(2)}) async-start(f32[128,16,128]{2,1,0:T(8,128)} %bitcast.15), calls=%async_computation | async-start | bytes 2097152 | tf_op jit(solution)/shard_map/all_to_all | solution.py:507
  18.4 0.0 copy-done.5
  18.4 0.7 collective-permute-start
  19.1 0.0 collective-permute-done.sigma_ref
  19.1 18.8 %all-to-all-done = f32[128,16,128]{2,1,0:T(8,128)S(1)} async-done(((f32[128,16,128]{2,1,0:T(8,128)}), f32[128,16,128]{2,1,0:T(8,128)S(1)}, u32[]{:S(2)}, u32[]{:S(2)}) %all-to-all-start) | async-done | bytes 1048608 | tf_op jit(solution)/shard_map/all_to_all | solution.py:507
  37.8 1.7 %block_sums.1 = (f32[128,1024]{1,0:T(8,128)S(1)}, f32[152,768]{1,0:T(8,128)S(1)}, f32[152,768]{1,0:T(8,128)S(1)}, s32[16,128]{1,0:T(8,128)S(1)}, f32[32,1024]{1,0:T(8,128)S(1)}) custom-call(f32[2048,128]{1,0:T(8,128)S(1)} %bitcast.13, f32[4,32,256]{2,1,0:T(8,128)S(1)} %collective-permute-done.sigma_ref), custom_call_target="tpu_custom_call" | custom-call | flops 1100000000 | bytes 5000000 | tf_op jit(solution)/shard_map/block_sums/pallas_call | solution.py:271
  39.6 1.0 %collective-permute-start.1 = (f32[152,768]{1,0:T(8,128)S(1)}, f32[152,768]{1,0:T(8,128)S(1)}, u32[]{:S(2)}, u32[]{:S(2)}) collective-permute-start(f32[152,768]{1,0:T(8,128)S(1)} %get-tuple-element.14), channel_id=1, source_target_pairs={{0,97},{1,2},{2,1},{3,4},{4,3},{5,6},{6,5},{7,14},{14,7},{15,12},{... | collective-permute-start | bytes 1400840 | tf_op jit(solution)/shard_map/ppermute | solution.py:520
  40.6 2.2 %collective-permute-start.2 = (f32[152,768]{1,0:T(8,128)S(1)}, f32[152,768]{1,0:T(8,128)S(1)}, u32[]{:S(2)}, u32[]{:S(2)}) collective-permute-start(f32[152,768]{1,0:T(8,128)S(1)} %get-tuple-element.15), channel_id=1, source_target_pairs={{0,1},{1,0},{2,3},{3,2},{4,5},{5,4},{6,7},{7,6},{14,15},{15,14},{1... | collective-permute-start | bytes 1400840 | tf_op jit(solution)/shard_map/ppermute | solution.py:521
  42.7 5.2 %collective-permute-done.1.far_ref = f32[152,768]{1,0:T(8,128)S(1)} collective-permute-done((f32[152,768]{1,0:T(8,128)S(1)}, f32[152,768]{1,0:T(8,128)S(1)}, u32[]{:S(2)}, u32[]{:S(2)}) %collective-permute-start.1) | collective-permute-done | bytes 466976 | tf_op jit(solution)/shard_map/ppermute | solution.py:520
  47.9 0.0 collective-permute-done.2.near_ref
  47.9 3.4 %sweeps.1 = f32[2048,128]{1,0:T(8,128)S(1)} custom-call(f32[128,1024]{1,0:T(8,128)S(1)} %get-tuple-element.13.own_ref, f32[152,768]{1,0:T(8,128)S(1)} %collective-permute-done.1.far_ref, f32[152,768]{1,0:T(8,128)S(1)} %collective-permute-done.2.near_ref, f32[32,1024]{1,0:T(8,128)S(1)} %get-tuple-element.16.sig_ref, s32[16,128]{1,0:T(8,128)S(1)} %get-tuple-element.17.from_ref), custom_call_target="tpu_custom_call" | custom-call | tf_op jit(solution)/shard_map/sweeps/pallas_call | solution.py:418
  51.3 0.0 copy-start
  51.3 0.0 copy-start.1
  51.4 0.0 copy-start.2
  51.4 0.0 copy-start.3
  51.4 0.0 copy-start.4
  51.4 24.1 %all_to_all.10 = f32[128,16,128]{2,1,0:T(8,128)S(1)} all-to-all(f32[128,16,128]{2,1,0:T(8,128)S(1)} %bitcast.9), channel_id=1, replica_groups=mesh['edge'=16,'node'=8] {'edge','node'}, dimensions={0} | all-to-all | bytes 2097152 | tf_op jit(solution)/shard_map/all_to_all | solution.py:507
  75.5 0.0 copy-done
  75.5 0.0 copy-done.1
  75.5 0.0 copy-done.2
  75.5 0.0 copy-done.3
  75.5 0.0 copy-done.4
  75.5 2.7 %lift.1 = f32[64,1024]{1,0:T(8,128)} custom-call(f32[2048,128]{1,0:T(8,128)S(1)} %bitcast.10, s32[1,1024]{1,0:T(1,128)S(1)} %copy-done.4, f32[64,1024]{1,0:T(8,128)S(1)} %copy-done.2, f32[3,64,1024]{2,1,0:T(8,128)S(1)} %copy-done, f32[64,1024]{1,0:T(8,128)S(1)} %copy-done.3, s32[2,64,1024]{2,1,0:T(8,128)S(1)} %copy-done.1), custom_call_target="tpu_custom_call" | custom-call | tf_op jit(solution)/shard_map/lift/pallas_call | solution.py:489
Async XLA Ops:
  6.8 11.5 %copy-start.5 = (f32[4,32,256]{2,1,0:T(8,128)S(1)}, f32[4,32,256]{2,1,0:T(8,128)}, u32[]{:S(2)}) copy-start(f32[4,32,256]{2,1,0:T(8,128)} %param.13) | copy-start | bytes 393220
  6.9 31.0 %all-to-all-start = ((f32[128,16,128]{2,1,0:T(8,128)}), f32[128,16,128]{2,1,0:T(8,128)S(1)}, u32[]{:S(2)}, u32[]{:S(2)}) async-start(f32[128,16,128]{2,1,0:T(8,128)} %bitcast.15), calls=%async_computation | async-start | bytes 2097152 | tf_op jit(solution)/shard_map/all_to_all | solution.py:507
  18.4 0.7 collective-permute-start
  39.6 8.4 %collective-permute-start.1 = (f32[152,768]{1,0:T(8,128)S(1)}, f32[152,768]{1,0:T(8,128)S(1)}, u32[]{:S(2)}, u32[]{:S(2)}) collective-permute-start(f32[152,768]{1,0:T(8,128)S(1)} %get-tuple-element.14), channel_id=1, source_target_pairs={{0,97},{1,2},{2,1},{3,4},{4,3},{5,6},{6,5},{7,14},{14,7},{15,12},{... | collective-permute-start | bytes 1400840 | tf_op jit(solution)/shard_map/ppermute | solution.py:520
  40.6 7.4 %collective-permute-start.2 = (f32[152,768]{1,0:T(8,128)S(1)}, f32[152,768]{1,0:T(8,128)S(1)}, u32[]{:S(2)}, u32[]{:S(2)}) collective-permute-start(f32[152,768]{1,0:T(8,128)S(1)} %get-tuple-element.15), channel_id=1, source_target_pairs={{0,1},{1,0},{2,3},{3,2},{4,5},{5,4},{6,7},{7,6},{14,15},{15,14},{1... | collective-permute-start | bytes 1400840 | tf_op jit(solution)/shard_map/ppermute | solution.py:521
  51.3 24.2 %copy-start = (f32[3,64,1024]{2,1,0:T(8,128)S(1)}, f32[3,64,1024]{2,1,0:T(8,128)}, u32[]{:S(2)}) copy-start(f32[3,64,1024]{2,1,0:T(8,128)} %tan_ref.1) | copy-start | bytes 2359300
  51.3 24.2 %copy-start.1 = (s32[2,64,1024]{2,1,0:T(8,128)S(1)}, s32[2,64,1024]{2,1,0:T(8,128)}, u32[]{:S(2)}) copy-start(s32[2,64,1024]{2,1,0:T(8,128)} %ends_ref.1) | copy-start | bytes 1572868
  51.4 24.2 %copy-start.2 = (f32[64,1024]{1,0:T(8,128)S(1)}, f32[64,1024]{1,0:T(8,128)}, u32[]{:S(2)}) copy-start(f32[64,1024]{1,0:T(8,128)} %res_ref.1) | copy-start | bytes 786436
  51.4 24.2 %copy-start.3 = (f32[64,1024]{1,0:T(8,128)S(1)}, f32[64,1024]{1,0:T(8,128)}, u32[]{:S(2)}) copy-start(f32[64,1024]{1,0:T(8,128)} %jac_ref.1) | copy-start | bytes 786436
  51.4 24.2 %copy-start.4 = (s32[1,1024]{1,0:T(1,128)S(1)}, s32[1,1024]{1,0:T(1,128)}, u32[]{:S(2)}) copy-start(s32[1,1024]{1,0:T(1,128)} %get-tuple-element.18.slot_ref) | copy-start | bytes 12292

commit v4 on v3

--- a/solution.py
+++ b/solution.py
@@ -22,7 +22,8 @@
 RING = ("edge", "node")
 VMEM_LIMIT = 24 * 1024 * 1024
 FIRST_LIMIT = 60 * 1024 * 1024
-MESSAGE = ROW + 24
+MESSAGE = ROW + 16
+TILES = NODES // 8
 
 mass_scale = (1.0, 1.0, 1.0, 0.5)
 
@@ -229,166 +230,252 @@
     )
 
 
-def sums_kernel(got_ref, sigma_ref, own_ref, far_ref, near_ref, from_ref, sig_ref, rows_scr, hot_scr):
+def numbers(scalar):
+    centre, one, two = chebyshev_numbers(mass_scale[3 if scalar else 0])
+    return 1.0 / centre, one, two, mass_scale[3 if scalar else 0]
+
+
+def beside(here):
+    lane = iota((8, 128), 1)
+    row = iota((8, 128), 0)
+    low, high = (lane & 31) > 0, (lane & 31) < 31
+    bottom, top = row == 0, row == 7
+    up = [[pltpu.roll(value, 1, 0) for value in part] for part in here]
+    down = [[pltpu.roll(value, 7, 0) for value in part] for part in here]
+    first = [pltpu.roll(part[-1], 32, 1) for part in up]
+    last = [pltpu.roll(part[0], 96, 1) for part in down]
+    first = [jnp.where(lane < 32, 0.0, first[0]), jnp.where(lane < 32, first[0], first[1])]
+    last = [jnp.where(lane < 96, last[0], last[1]), jnp.where(lane < 96, last[1], 0.0)]
+    sums = []
+    for half in range(2):
+        sums.append([])
+        for tile in range(TILES):
+            below = up[half][tile - 1] if tile else first[half]
+            above = down[half][tile + 1] if tile < TILES - 1 else last[half]
+            axial = jnp.where(bottom, below, up[half][tile]) + jnp.where(top, above, down[half][tile])
+            value = here[half][tile]
+            inner = jnp.where(low, pltpu.roll(value, 1, 1), 0.0)
+            outer = jnp.where(high, pltpu.roll(value, 127, 1), 0.0)
+            sums[half].append((axial + inner) + outer)
+    return sums
+
+
+def spot(s, half):
+    return slice(s * SLICE + half * 128, s * SLICE + half * 128 + 128)
+
+
+def summed(rows_scr, hot):
+    both = dot(rows_scr[...], hot, ((1,), (0,)))
+    sums = both[:ROW] + both[ROW:]
+    first = iota((NODES, SLICE), 0) == 0
+    scalar = sums[LABEL:]
+    rest = -jnp.sum(jnp.where(first, 0.0, scalar), axis=0, keepdims=True)
+    return jnp.concatenate([sums[:LABEL], jnp.where(first, rest, scalar)], axis=0)
+
+
+def turned_label(label):
+    return (label.astype(I32) - 1) ^ (odd_slab() * 768)
+
+
+def first_sweep(source, sigma, store, s, inside):
+    for channel in range(4):
+        invert, one, two, mass = numbers(channel == 3)
+        here = [
+            [source(channel, s, half, tile) * invert for tile in range(TILES)] for half in range(2)
+        ]
+        near = beside(here)
+        for half in range(2):
+            for tile in range(TILES):
+                around = near[half][tile]
+                for other in inside:
+                    around = around + source(channel, other, half, tile) * invert
+                value = here[half][tile]
+                rest = source(channel, s, half, tile) - (
+                    (6.0 + mass * sigma(s, half, tile)) * value - around
+                )
+                store(channel, half, tile, value + (one * value + two * rest))
+
+
+def put_sigma(message_ref, sig_ref, s):
+    for tile in range(TILES):
+        at, lanes = ROW + tile // 3 * 8, slice(tile % 3 * SLICE, (tile % 3 + 1) * SLICE)
+        message_ref[at : at + 8, lanes] = sig_ref[tile * 8 : tile * 8 + 8, s * SLICE : (s + 1) * SLICE]
+    message_ref[ROW + 8 :, SLICE:] = jnp.zeros((8, 2 * SLICE), F32)
+
+
+def channel_rows(channel, tile):
+    at = channel * NODES + tile * 8
+    return slice(at, at + 8)
+
+
+def far_kernel(got_ref, sigma_ref, far_ref, mid_ref, from_ref, sig_ref, rows_scr, hot_scr):
+    for s in range(4):
+        turned = sigma_ref[s ^ (odd_slab() * 3)].T
+        for block in range(8):
+            at = s * SLICE + block * 32
+            sig_ref[:, at : at + 32] = turned[block * 32 : (block + 1) * 32, :]
     for step in range(SLOTS // 128):
         part = slice(step * 128, (step + 1) * 128)
         turned = got_ref[part, :].T
         high, low = split(turned)
         rows_scr[0:ROW, part] = high
         rows_scr[ROW:, part] = low
-        label = turned[LABEL : LABEL + 1, :].astype(I32)
-        from_ref[step : step + 1, :] = jnp.maximum(label - 1, 0)
-        column = got_ref[part, LABEL : LABEL + 1].astype(I32)
-        hot_scr[part, :] = one_hot(column == iota((128, BLOCKS), 1) + 1)
-
-    for step in range(BLOCKS // 256):
-        lanes = slice(step * 256, (step + 1) * 256)
-        both = dot(rows_scr[...], hot_scr[:, lanes], ((1,), (0,)))
-        sums = both[:ROW] + both[ROW:]
-        scalar = sums[LABEL:]
-        first = iota((NODES, 256), 0) == 0
-        rest = -jnp.sum(jnp.where(first, 0.0, scalar), axis=0, keepdims=True)
-        own_ref[0:LABEL, lanes] = sums[:LABEL]
-        own_ref[LABEL:, lanes] = jnp.where(first, rest, scalar)
-    for s in range(4):
-        turned = sigma_ref[s].T
-        for block in range(8):
-            at = s * SLICE + block * 32
-            sig_ref[:, at : at + 32] = turned[block * 32 : (block + 1) * 32, :]
-    odd = odd_slab()
-    for ref, after in ((far_ref, odd), (near_ref, 1 - odd)):
-        ref[0:ROW, :] = own_ref[:, pl.ds(pl.multiple_of(after * SLICE, SLICE), HALO)]
-        lanes = pl.ds(pl.multiple_of(after * (2 * SLICE), 2 * SLICE), 2 * SLICE)
-        ref[ROW:, 0 : 2 * SLICE] = sig_ref[0:24, lanes]
-        for s in range(2):
-            lanes = pl.ds(pl.multiple_of((2 * after + s) * SLICE, SLICE), SLICE)
-            ref[ROW + 8 * s : ROW + 8 * s + 8, 2 * SLICE :] = sig_ref[24:, lanes]
-        ref[ROW + 16 :, 2 * SLICE :] = jnp.zeros((8, SLICE), F32)
-
-
-def block_sums(got, sigma):
+        from_ref[step : step + 1, :] = jnp.maximum(turned_label(turned[LABEL : LABEL + 1, :]), 0)
+        column = turned_label(got_ref[part, LABEL : LABEL + 1])
+        hot_scr[part, :] = one_hot(column == iota((128, HALO), 1))
+
+    def source(channel, s, half, tile):
+        if s == 0:
+            return far_ref[channel_rows(channel, tile), spot(0, half)]
+        return mid_ref[channel_rows(channel, tile), spot(s - 1, half)]
+
+    def sigma(s, half, tile):
+        return sig_ref[tile * 8 : tile * 8 + 8, spot(s, half)]
+
+    def store(s):
+        def one(channel, half, tile, value):
+            far_ref[channel_rows(channel, tile), spot(1 + s, half)] = value
+
+        return one
+
+    for s in range(3):
+        sums = summed(rows_scr, hot_scr[:, s * SLICE : (s + 1) * SLICE])
+        if s == 0:
+            far_ref[0:ROW, 0:SLICE] = sums
+        else:
+            mid_ref[:, (s - 1) * SLICE : s * SLICE] = sums
+    first_sweep(source, sigma, store(0), 0, (1,))
+    first_sweep(source, sigma, store(1), 1, (0, 2))
+    put_sigma(far_ref, sig_ref, 0)
+
+
+def far_sums(got, sigma):
     vmem = pl.BlockSpec(memory_space=pltpu.VMEM)
     return pl.pallas_call(
-        sums_kernel,
+        far_kernel,
         out_shape=(
-            jax.ShapeDtypeStruct((ROW, BLOCKS), F32),
             jax.ShapeDtypeStruct((MESSAGE, HALO), F32),
-            jax.ShapeDtypeStruct((MESSAGE, HALO), F32),
+            jax.ShapeDtypeStruct((ROW, 2 * SLICE), F32),
             jax.ShapeDtypeStruct((SLOTS // 128, 128), I32),
             jax.ShapeDtypeStruct((NODES, BLOCKS), F32),
         ),
         in_specs=[vmem] * 2,
-        out_specs=[vmem] * 5,
+        out_specs=[vmem] * 4,
         scratch_shapes=[
             pltpu.VMEM((2 * ROW, SLOTS), BF16),
-            pltpu.VMEM((SLOTS, BLOCKS), BF16),
+            pltpu.VMEM((SLOTS, HALO), BF16),
         ],
         compiler_params=pltpu.CompilerParams(vmem_limit_bytes=VMEM_LIMIT),
-        cost_estimate=pl.CostEstimate(flops=1_100_000_000, bytes_accessed=5_000_000, transcendentals=0),
-        name="block_sums",
+        cost_estimate=pl.CostEstimate(flops=800_000_000, bytes_accessed=5_000_000, transcendentals=0),
+        name="far_sums",
     )(got, sigma)
 
 
+def near_kernel(got_ref, mid_ref, sig_ref, near_ref, rows_scr, hot_scr):
+    for step in range(SLOTS // 128):
+        part = slice(step * 128, (step + 1) * 128)
+        high, low = split(got_ref[part, :].T)
+        rows_scr[0:ROW, part] = high
+        rows_scr[ROW:, part] = low
+        column = turned_label(got_ref[part, LABEL : LABEL + 1])
+        hot_scr[part, :] = one_hot(column == iota((128, SLICE), 1) + HALO)
+
+    def source(channel, s, half, tile):
+        if s == 3:
+            return near_ref[channel_rows(channel, tile), spot(0, half)]
+        return mid_ref[channel_rows(channel, tile), spot(s - 1, half)]
+
+    def sigma(s, half, tile):
+        return sig_ref[tile * 8 : tile * 8 + 8, spot(s, half)]
+
+    def store(s):
+        def one(channel, half, tile, value):
+            near_ref[channel_rows(channel, tile), spot(4 - s, half)] = value
+
+        return one
+
+    near_ref[0:ROW, 0:SLICE] = summed(rows_scr, hot_scr[...])
+    first_sweep(source, sigma, store(3), 3, (2,))
+    first_sweep(source, sigma, store(2), 2, (1, 3))
+    put_sigma(near_ref, sig_ref, 3)
+
+
+def near_sums(got, mid, sig):
+    vmem = pl.BlockSpec(memory_space=pltpu.VMEM)
+    return pl.pallas_call(
+        near_kernel,
+        out_shape=jax.ShapeDtypeStruct((MESSAGE, HALO), F32),
+        in_specs=[vmem] * 3,
+        out_specs=vmem,
+        scratch_shapes=[
+            pltpu.VMEM((2 * ROW, SLOTS), BF16),
+            pltpu.VMEM((SLOTS, SLICE), BF16),
+        ],
+        compiler_params=pltpu.CompilerParams(vmem_limit_bytes=VMEM_LIMIT),
+        cost_estimate=pl.CostEstimate(flops=300_000_000, bytes_accessed=4_000_000, transcendentals=0),
+        name="near_sums",
+    )(got, mid, sig)
+
+
 def sweeps_kernel(
-    own_ref, far_ref, near_ref, sig_ref, from_ref, back_ref,
-    diag_scr, d_scr, y_scr, p_scr, keep_scr, sol_scr, row_scr, place_scr, place_sem,
+    far_ref, near_ref, mid_ref, before_ref, after_ref, sig_ref, from_ref, back_ref,
+    diag_scr, y_scr, p_scr, keep_scr, sol_scr, row_scr, place_scr, place_sem,
 ):
     to_scalar = pltpu.make_async_copy(from_ref, place_scr, place_sem)
     to_scalar.start()
-    odd = odd_slab() == 1
-
-    def halo(behind, index):
-        far, near = far_ref[index], near_ref[index]
-        return jnp.where(odd, near, far) if behind else jnp.where(odd, far, near)
-
-    tiles = NODES // 8
-    lane = iota((8, 128), 1)
-    row = iota((8, 128), 0)
-    low, high = (lane & 31) > 0, (lane & 31) < 31
-    bottom, top = row == 0, row == 7
 
     def put(scr, s, half, tile, value):
-        scr[s + 3, half, tile * 8 : tile * 8 + 8, :] = value
+        scr[s + 2, half, tile * 8 : tile * 8 + 8, :] = value
 
     def get(scr, s, half, tile):
-        return scr[s + 3, half, tile * 8 : tile * 8 + 8, :]
-
-    def beside(scr, s):
-        here = [[get(scr, s, half, tile) for tile in range(tiles)] for half in range(2)]
-        up = [[pltpu.roll(value, 1, 0) for value in part] for part in here]
-        down = [[pltpu.roll(value, 7, 0) for value in part] for part in here]
-        first = [pltpu.roll(part[-1], 32, 1) for part in up]
-        last = [pltpu.roll(part[0], 96, 1) for part in down]
-        first = [jnp.where(lane < 32, 0.0, first[0]), jnp.where(lane < 32, first[0], first[1])]
-        last = [jnp.where(lane < 96, last[0], last[1]), jnp.where(lane < 96, last[1], 0.0)]
-        sums = []
+        return scr[s + 2, half, tile * 8 : tile * 8 + 8, :]
+
+    def apply(scr, s, kind):
+        near = beside([[get(scr, s, half, tile) for tile in range(TILES)] for half in range(2)])
         for half in range(2):
-            sums.append([])
-            for tile in range(tiles):
-                below = up[half][tile - 1] if tile else first[half]
-                above = down[half][tile + 1] if tile < tiles - 1 else last[half]
-                axial = jnp.where(bottom, below, up[half][tile]) + jnp.where(top, above, down[half][tile])
-                value = here[half][tile]
-                inner = jnp.where(low, pltpu.roll(value, 1, 1), 0.0)
-                outer = jnp.where(high, pltpu.roll(value, 127, 1), 0.0)
-                sums[half].append((axial + inner) + outer)
-        return sums
-
-    def apply(scr, s, kind):
-        near = beside(scr, s)
-        for half in range(2):
-            for tile in range(tiles):
+            for tile in range(TILES):
                 here = get(scr, s, half, tile)
                 beyond = get(scr, s - 1, half, tile) + get(scr, s + 1, half, tile)
-                diag = diag_scr[kind, s + 2, half, tile * 8 : tile * 8 + 8, :]
+                diag = diag_scr[kind, s + 1, half, tile * 8 : tile * 8 + 8, :]
                 yield half, tile, here, diag * here - (beyond + near[half][tile])
 
-    def keep_diag(s, half, rows, sig):
-        for i, mass in enumerate((mass_scale[0], mass_scale[3])):
-            diag_scr[i, s + 2, half, rows, :] = 6.0 + mass * sig
-
-    every, upper, lower = slice(0, NODES), slice(0, 24), slice(24, NODES)
     for half in range(2):
-        for s in range(4):
-            keep_diag(s, half, every, sig_ref[:, s * SLICE + half * 128 : s * SLICE + half * 128 + 128])
-        for behind, first in ((True, -2), (False, 4)):
-            for s in range(2):
-                at = s * SLICE + half * 128
-                sig = halo(behind, (slice(ROW, ROW + 24), slice(at, at + 128)))
-                keep_diag(first + s, half, upper, sig)
-                at = 2 * SLICE + half * 128
-                sig = halo(behind, (slice(ROW + 8 * s, ROW + 8 * s + 8), slice(at, at + 128)))
-                keep_diag(first + s, half, lower, sig)
+        for tile in range(TILES):
+            nodes = slice(tile * 8, tile * 8 + 8)
+            at = ROW + tile // 3 * 8
+            for s in range(-1, 5):
+                if 0 <= s < 4:
+                    sigma = sig_ref[nodes, spot(s, half)]
+                else:
+                    sigma = (before_ref if s < 0 else after_ref)[at : at + 8, spot(tile % 3, half)]
+                for i, mass in enumerate((mass_scale[0], mass_scale[3])):
+                    diag_scr[i, s + 1, half, nodes, :] = 6.0 + mass * sigma
 
     def channel_step(channel, _):
         scalar = channel == 3
-        vector_numbers = chebyshev_numbers(mass_scale[0])
-        scalar_numbers = chebyshev_numbers(mass_scale[3])
-        _, one, two = [
-            jnp.where(scalar, b, a).astype(F32) for a, b in zip(vector_numbers, scalar_numbers)
+        invert, one, two, _ = [
+            jnp.where(scalar, b, a).astype(F32) for a, b in zip(numbers(False), numbers(True))
         ]
-        invert = jnp.where(scalar, 1.0 / scalar_numbers[0], 1.0 / vector_numbers[0]).astype(F32)
         kind = jnp.where(scalar, 1, 0)
         base = channel * NODES
+        across = two * invert
 
         def rows(tile):
             return pl.ds(pl.multiple_of(base + tile * 8, 8), 8)
 
         def source(s, half, tile):
-            behind, beyond = s < 0, s < 0 or s > 3
-            if beyond:
-                s = s + 3 if behind else s - 4
-            index = (rows(tile), slice(s * SLICE + half * 128, s * SLICE + half * 128 + 128))
-            return halo(behind, index) if beyond else own_ref[index]
-
-        for s in range(-3, 7):
-            for half in range(2):
-                for tile in range(tiles):
-                    put(d_scr, s, half, tile, source(s, half, tile) * invert)
-        for s in range(-2, 6):
-            for half, tile, here, applied in apply(d_scr, s, kind):
-                rest = source(s, half, tile) - applied
-                put(y_scr, s, half, tile, here + (one * here + two * rest))
+            if s in (1, 2):
+                return mid_ref[rows(tile), spot(s - 1, half)]
+            ref = {-1: before_ref, 0: far_ref, 3: near_ref, 4: after_ref}[s]
+            return ref[rows(tile), spot(0, half)]
+
+        for half in range(2):
+            for tile in range(TILES):
+                for s, ref, beyond in ((0, far_ref, -1), (3, near_ref, 4), (-1, before_ref, 0), (4, after_ref, 3)):
+                    part = ref[rows(tile), spot(1, half)]
+                    put(y_scr, s, half, tile, part + across * source(beyond, half, tile))
+                for s, ref in ((1, far_ref), (2, near_ref), (-2, before_ref), (5, after_ref)):
+                    put(y_scr, s, half, tile, ref[rows(tile), spot(2, half)])
         for s in range(-1, 5):
             for half, tile, here, applied in apply(y_scr, s, kind):
                 rest = source(s, half, tile) - applied
@@ -398,9 +485,8 @@
         for s in range(4):
             for half, tile, here, applied in apply(p_scr, s, kind):
                 rest = keep_scr[s, half, tile * 8 : tile * 8 + 8, :] - applied
-                at = s * SLICE + half * 128
                 value = (get(y_scr, s, half, tile) + here) + (one * here + two * rest)
-                sol_scr[rows(tile), at : at + 128] = value
+                sol_scr[rows(tile), spot(s, half)] = value
         return 0
 
     lax.fori_loop(0, 4, channel_step, 0)
@@ -412,17 +498,16 @@
         back_ref[slot : slot + 1, :] = row_scr[pl.ds(place_scr[slot // 128, slot % 128], 1), :]
 
 
-def sweeps(own, far, near, sig, labels):
+def sweeps(far, near, mid, before, after, sig, labels):
     vmem = pl.BlockSpec(memory_space=pltpu.VMEM)
-    field = pltpu.VMEM((10, 2, NODES, 128), F32)
+    field = pltpu.VMEM((8, 2, NODES, 128), F32)
     return pl.pallas_call(
         sweeps_kernel,
         out_shape=jax.ShapeDtypeStruct((SLOTS, ROW), F32),
-        in_specs=[vmem] * 5,
+        in_specs=[vmem] * 7,
         out_specs=vmem,
         scratch_shapes=[
-            pltpu.VMEM((2, 8, 2, NODES, 128), F32),
-            field,
+            pltpu.VMEM((2, 6, 2, NODES, 128), F32),
             field,
             field,
             pltpu.VMEM((4, 2, NODES, 128), F32),
@@ -433,7 +518,7 @@
         ],
         compiler_params=pltpu.CompilerParams(vmem_limit_bytes=VMEM_LIMIT),
         name="sweeps",
-    )(own, far, near, sig, labels)
+    )(far, near, mid, before, after, sig, labels)
 
 
 def lift_kernel(got_ref, slot_ref, res_ref, tan_ref, jac_ref, ends_ref, out_hbm, row_scr, y_scr, out_ref, out_sem):
@@ -516,10 +601,11 @@
         residual, tangent, ends, target.reshape(1, BLOCKS), node_block.reshape(1, BLOCKS)
     )
     got = exchange(send)
-    own, far, near, labels, sig = block_sums(got, sig_own)
-    far = lax.ppermute(far, RING, between)
-    near = lax.ppermute(near, RING, within)
-    back = sweeps(own, far, near, sig, labels)
+    far, mid, labels, sig = far_sums(got, sig_own)
+    before = lax.ppermute(far, RING, between)
+    near = near_sums(got, mid, sig)
+    after = lax.ppermute(near, RING, within)
+    back = sweeps(far, near, mid, before, after, sig, labels)
     mine = exchange(back)
     return lift(mine, slots, residual, tangent, jacobi, ends)
 

time: 78.5 us -> 77.4 us (0.986)
  waiting for transfers between devices: 24 us -> 22.5 us
    ppermute x2, waiting for transfers between devices: 5.2 us -> 3.75 us  [the longest x1 3.75 us: per_device(): before = lax.ppermute(far, RING, between)]
    pallas_call x1 -> x2, Pallas kernels: 1.72 us -> 2.87 us  [the longest x1 1.77 us: far_sums(): pl.pallas_call(far_kernel, out_shape=(jax.ShapeDtypeStruct((MESSAGE, HALO...]
    pallas_call x1, Pallas kernels: 3.39 us -> 2.56 us  [sweeps(): pl.pallas_call(sweeps_kernel, out_shape=jax.ShapeDtypeStruct((SLOTS, ROW)...]
  transfers between devices with their start and end apart: 4 -> 4, of which waited for: 2 -> 2; matrix products, arithmetic and copies ran while one was open for 0% -> 0% of each run, Pallas kernels for 0% -> 1%
where the time goes in v4:
time: 77.4 us; the launch traced here: 77.2 us
  blocking collectives  24.1 us (31%)
  waiting for transfers between devices  22.5 us (29%)
  starting transfers between devices  15.4 us (20%)
  Pallas kernels  15 us (19%)
    all_to_all x1, blocking collectives, exchange(): lax.all_to_all(parts, RING, split_axis=0, concat_axis=0, tiled=True)  24.1 us
    all_to_all x1, waiting for transfers between devices, exchange(): lax.all_to_all(parts, RING, split_axis=0, concat_axis=0, tiled=True)  18.8 us
    all_to_all x1, starting transfers between devices, exchange(): lax.all_to_all(parts, RING, split_axis=0, concat_axis=0, tiled=True)  11.5 us
    pallas_call x1, Pallas kernels, edge_terms(): pl.pallas_call(terms_kernel, out_shape=(jax.ShapeDtypeStruct((SLOTS, ROW)...  6.83 us
    ppermute x1, waiting for transfers between devices, per_device(): before = lax.ppermute(far, RING, between)  3.75 us
    pallas_call x1, Pallas kernels, lift(): pl.pallas_call(lift_kernel, out_shape=jax.ShapeDtypeStruct((EDGES, BLOCKS...  2.7 us
    pallas_call x1, Pallas kernels, sweeps(): pl.pallas_call(sweeps_kernel, out_shape=jax.ShapeDtypeStruct((SLOTS, ROW)...  2.56 us
    ppermute x1, starting transfers between devices, per_device(): after = lax.ppermute(near, RING, within)  2.24 us
  transfers between devices with their start and end apart: 4, of which 2 were waited for; matrix products, arithmetic and copies ran while one was open for 0% of the time, Pallas kernels for 1%

profile of v4, /device:TPU:1, one launch (start us, length us, event | category | flops | bytes accessed | tf_op | source)
XLA Modules:
  0.0 77.2 jit_solution(15146014986607828128)
XLA Ops:
  0.0 6.8 %edge_terms.1 = (f32[2048,128]{1,0:T(8,128)}, s32[1,1024]{1,0:T(1,128)}) custom-call(s32[1,1024]{1,0:T(1,128)} %bitcast.17, s32[1,1024]{1,0:T(1,128)} %bitcast.18, f32[8,8,1024]{2,1,0:T(8,128)} %bitcast.15, f32[3,8,8,1024]{3,2,1,0:T(8,128)} %bitcast.13, s32[2,8,8,1024]{3,2,1,0:T(8,128)} %bitcast.14), custom_call_target="tpu_custom_call" | custom-call | flops 50000000 | bytes 20000000 | tf_op jit(solution)/shard_map/edge_terms/pallas_call | solution.py:195
  6.8 0.0 copy-start.5
  6.9 11.5 %all-to-all-start = ((f32[128,16,128]{2,1,0:T(8,128)}), f32[128,16,128]{2,1,0:T(8,128)S(1)}, u32[]{:S(2)}, u32[]{:S(2)}) async-start(f32[128,16,128]{2,1,0:T(8,128)} %bitcast.16), calls=%async_computation | async-start | bytes 2097152 | tf_op jit(solution)/shard_map/all_to_all | solution.py:592
  18.4 0.0 copy-done.5
  18.4 0.7 collective-permute-start
  19.1 0.0 collective-permute-done.sigma_ref
  19.1 18.8 %all-to-all-done = f32[128,16,128]{2,1,0:T(8,128)S(1)} async-done(((f32[128,16,128]{2,1,0:T(8,128)}), f32[128,16,128]{2,1,0:T(8,128)S(1)}, u32[]{:S(2)}, u32[]{:S(2)}) %all-to-all-start) | async-done | bytes 1048608 | tf_op jit(solution)/shard_map/all_to_all | solution.py:592
  37.8 1.8 %far_sums.1 = (f32[144,768]{1,0:T(8,128)S(1)}, f32[128,512]{1,0:T(8,128)S(1)}, s32[16,128]{1,0:T(8,128)S(1)}, f32[32,1024]{1,0:T(8,128)S(1)}) custom-call(f32[2048,128]{1,0:T(8,128)S(1)} %bitcast.10, f32[4,32,256]{2,1,0:T(8,128)S(1)} %collective-permute-done.sigma_ref), custom_call_target="tpu_custom_call" | custom-call | flops 800000000 | bytes 5000000 | tf_op jit(solution)/shard_map/far_sums/pallas_call | solution.py:354
  39.6 1.0 %collective-permute-start.1 = (f32[144,768]{1,0:T(8,128)S(1)}, f32[144,768]{1,0:T(8,128)S(1)}, u32[]{:S(2)}, u32[]{:S(2)}) collective-permute-start(f32[144,768]{1,0:T(8,128)S(1)} %get-tuple-element.12.far_ref), channel_id=1, source_target_pairs={{0,97},{1,2},{2,1},{3,4},{4,3},{5,6},{6,5},{7,14},{14,7},{15,12},{... | collective-permute-start | bytes 1327112 | tf_op jit(solution)/shard_map/ppermute | solution.py:605
  40.6 1.1 %near_sums.1.near_ref = f32[144,768]{1,0:T(8,128)S(1)} custom-call(f32[2048,128]{1,0:T(8,128)S(1)} %bitcast.11, f32[128,512]{1,0:T(8,128)S(1)} %get-tuple-element.13.mid_ref, f32[32,1024]{1,0:T(8,128)S(1)} %get-tuple-element.14.sig_ref), custom_call_target="tpu_custom_call" | custom-call | flops 300000000 | bytes 4000000 | tf_op jit(solution)/shard_map/near_sums/pallas_call | solution.py:405
  41.7 2.2 %collective-permute-start.2 = (f32[144,768]{1,0:T(8,128)S(1)}, f32[144,768]{1,0:T(8,128)S(1)}, u32[]{:S(2)}, u32[]{:S(2)}) collective-permute-start(f32[144,768]{1,0:T(8,128)S(1)} %near_sums.1.near_ref), channel_id=1, source_target_pairs={{0,1},{1,0},{2,3},{3,2},{4,5},{5,4},{6,7},{7,6},{14,15},{15,14},{1... | collective-permute-start | bytes 1327112 | tf_op jit(solution)/shard_map/ppermute | solution.py:607
  44.0 3.7 %collective-permute-done.1.before_ref = f32[144,768]{1,0:T(8,128)S(1)} collective-permute-done((f32[144,768]{1,0:T(8,128)S(1)}, f32[144,768]{1,0:T(8,128)S(1)}, u32[]{:S(2)}, u32[]{:S(2)}) %collective-permute-start.1) | collective-permute-done | bytes 442400 | tf_op jit(solution)/shard_map/ppermute | solution.py:605
  47.7 0.0 collective-permute-done.2.after_ref
  47.7 2.6 %sweeps.1 = f32[2048,128]{1,0:T(8,128)S(1)} custom-call(f32[144,768]{1,0:T(8,128)S(1)} %get-tuple-element.12.far_ref, f32[144,768]{1,0:T(8,128)S(1)} %near_sums.1.near_ref, f32[128,512]{1,0:T(8,128)S(1)} %get-tuple-element.13.mid_ref, f32[144,768]{1,0:T(8,128)S(1)} %collective-permute-done.1.before_ref, f32[144,768]{1,0:T(8,128)S(1)} %collective-permute-done.2.after_ref, ...), custom_call_target="tpu_custom_call" | custom-call | tf_op jit(solution)/shard_map/sweeps/pallas_call | solution.py:504
  50.3 0.0 copy-start
  50.3 0.0 copy-start.1
  50.3 0.0 copy-start.2
  50.3 0.0 copy-start.3
  50.3 0.0 copy-start.4
  50.4 24.1 %all_to_all.10 = f32[128,16,128]{2,1,0:T(8,128)S(1)} all-to-all(f32[128,16,128]{2,1,0:T(8,128)S(1)} %bitcast.9), channel_id=1, replica_groups=mesh['edge'=16,'node'=8] {'edge','node'}, dimensions={0} | all-to-all | bytes 2097152 | tf_op jit(solution)/shard_map/all_to_all | solution.py:592
  74.5 0.0 copy-done
  74.5 0.0 copy-done.1
  74.5 0.0 copy-done.2
  74.5 0.0 copy-done.3
  74.5 0.0 copy-done.4
  74.5 2.7 %lift.1 = f32[64,1024]{1,0:T(8,128)} custom-call(f32[2048,128]{1,0:T(8,128)S(1)} %bitcast.12, s32[1,1024]{1,0:T(1,128)S(1)} %copy-done.4, f32[64,1024]{1,0:T(8,128)S(1)} %copy-done.2, f32[3,64,1024]{2,1,0:T(8,128)S(1)} %copy-done, f32[64,1024]{1,0:T(8,128)S(1)} %copy-done.3, s32[2,64,1024]{2,1,0:T(8,128)S(1)} %copy-done.1), custom_call_target="tpu_custom_call" | custom-call | tf_op jit(solution)/shard_map/lift/pallas_call | solution.py:574
Async XLA Ops:
  6.8 11.5 %copy-start.5 = (f32[4,32,256]{2,1,0:T(8,128)S(1)}, f32[4,32,256]{2,1,0:T(8,128)}, u32[]{:S(2)}) copy-start(f32[4,32,256]{2,1,0:T(8,128)} %param.13) | copy-start | bytes 393220
  6.9 31.0 %all-to-all-start = ((f32[128,16,128]{2,1,0:T(8,128)}), f32[128,16,128]{2,1,0:T(8,128)S(1)}, u32[]{:S(2)}, u32[]{:S(2)}) async-start(f32[128,16,128]{2,1,0:T(8,128)} %bitcast.16), calls=%async_computation | async-start | bytes 2097152 | tf_op jit(solution)/shard_map/all_to_all | solution.py:592
  18.4 0.7 collective-permute-start
  39.6 8.1 %collective-permute-start.1 = (f32[144,768]{1,0:T(8,128)S(1)}, f32[144,768]{1,0:T(8,128)S(1)}, u32[]{:S(2)}, u32[]{:S(2)}) collective-permute-start(f32[144,768]{1,0:T(8,128)S(1)} %get-tuple-element.12.far_ref), channel_id=1, source_target_pairs={{0,97},{1,2},{2,1},{3,4},{4,3},{5,6},{6,5},{7,14},{14,7},{15,12},{... | collective-permute-start | bytes 1327112 | tf_op jit(solution)/shard_map/ppermute | solution.py:605
  41.7 6.0 %collective-permute-start.2 = (f32[144,768]{1,0:T(8,128)S(1)}, f32[144,768]{1,0:T(8,128)S(1)}, u32[]{:S(2)}, u32[]{:S(2)}) collective-permute-start(f32[144,768]{1,0:T(8,128)S(1)} %near_sums.1.near_ref), channel_id=1, source_target_pairs={{0,1},{1,0},{2,3},{3,2},{4,5},{5,4},{6,7},{7,6},{14,15},{15,14},{1... | collective-permute-start | bytes 1327112 | tf_op jit(solution)/shard_map/ppermute | solution.py:607
  50.3 24.2 %copy-start = (f32[3,64,1024]{2,1,0:T(8,128)S(1)}, f32[3,64,1024]{2,1,0:T(8,128)}, u32[]{:S(2)}) copy-start(f32[3,64,1024]{2,1,0:T(8,128)} %tan_ref.1) | copy-start | bytes 2359300
  50.3 24.2 %copy-start.1 = (s32[2,64,1024]{2,1,0:T(8,128)S(1)}, s32[2,64,1024]{2,1,0:T(8,128)}, u32[]{:S(2)}) copy-start(s32[2,64,1024]{2,1,0:T(8,128)} %ends_ref.1) | copy-start | bytes 1572868
  50.3 24.2 %copy-start.2 = (f32[64,1024]{1,0:T(8,128)S(1)}, f32[64,1024]{1,0:T(8,128)}, u32[]{:S(2)}) copy-start(f32[64,1024]{1,0:T(8,128)} %res_ref.1) | copy-start | bytes 786436
  50.3 24.2 %copy-start.3 = (f32[64,1024]{1,0:T(8,128)S(1)}, f32[64,1024]{1,0:T(8,128)}, u32[]{:S(2)}) copy-start(f32[64,1024]{1,0:T(8,128)} %jac_ref.1) | copy-start | bytes 786436
  50.3 24.2 %copy-start.4 = (s32[1,1024]{1,0:T(1,128)S(1)}, s32[1,1024]{1,0:T(1,128)}, u32[]{:S(2)}) copy-start(s32[1,1024]{1,0:T(1,128)} %get-tuple-element.16.slot_ref) | copy-start | bytes 12292

commit v5 on v4

--- a/solution.py
+++ b/solution.py
@@ -119,16 +119,18 @@
         term_scr[...] = 0.5 * tan_scr[:, :, :, lanes] * res_scr[:, :, lanes][None]
         if turned:
             turn(group - 1)
-        if posted:
-            post(group - 2, 0)
-        sums = edge_step(0, lanes, (jnp.zeros((NODES, 128), F32),) * 4)
+        sums = (jnp.zeros((NODES, 128), F32),) * 4
+        for step in range(3):
+            if posted:
+                post(group - 2, step)
+            sums = edge_step(step, lanes, sums)
 
         def tile_step(step, sums):
             if posted:
                 post(group - 2, step)
             return edge_step(step, lanes, sums)
 
-        sums = lax.fori_loop(1, EDGES // 8, tile_step, sums)
+        sums = lax.fori_loop(3, EDGES // 8, tile_step, sums)
         for channel in range(3):
             acc_scr[group, channel * NODES : (channel + 1) * NODES, :] = sums[channel]
         acc_scr[group, LABEL:, :] = sums[3]

time: 77.4 us -> 77.1 us (level)
  no operation moved by 1% of the time
where the time goes in v5:
time: 77.1 us; the launch traced here: 76.9 us
  blocking collectives  24.1 us (31%)
  waiting for transfers between devices  22.5 us (29%)
  starting transfers between devices  15.4 us (20%)
  Pallas kernels  14.6 us (19%)
    all_to_all x1, blocking collectives, exchange(): lax.all_to_all(parts, RING, split_axis=0, concat_axis=0, tiled=True)  24.1 us
    all_to_all x1, waiting for transfers between devices, exchange(): lax.all_to_all(parts, RING, split_axis=0, concat_axis=0, tiled=True)  18.8 us
    all_to_all x1, starting transfers between devices, exchange(): lax.all_to_all(parts, RING, split_axis=0, concat_axis=0, tiled=True)  11.5 us
    pallas_call x1, Pallas kernels, edge_terms(): pl.pallas_call(terms_kernel, out_shape=(jax.ShapeDtypeStruct((SLOTS, ROW)...  6.52 us
    ppermute x1, waiting for transfers between devices, per_device(): before = lax.ppermute(far, RING, between)  3.75 us
    pallas_call x1, Pallas kernels, lift(): pl.pallas_call(lift_kernel, out_shape=jax.ShapeDtypeStruct((EDGES, BLOCKS...  2.7 us
    pallas_call x1, Pallas kernels, sweeps(): pl.pallas_call(sweeps_kernel, out_shape=jax.ShapeDtypeStruct((SLOTS, ROW)...  2.56 us
    ppermute x1, starting transfers between devices, per_device(): after = lax.ppermute(near, RING, within)  2.24 us
  transfers between devices with their start and end apart: 4, of which 2 were waited for; matrix products, arithmetic and copies ran while one was open for 0% of the time, Pallas kernels for 1%

profile of v5, /device:TPU:1, one launch (start us, length us, event | category | flops | bytes accessed | tf_op | source)
XLA Modules:
  0.0 76.9 jit_solution(89724821421310672)
XLA Ops:
  0.0 6.5 %edge_terms.1 = (f32[2048,128]{1,0:T(8,128)}, s32[1,1024]{1,0:T(1,128)}) custom-call(s32[1,1024]{1,0:T(1,128)} %bitcast.17, s32[1,1024]{1,0:T(1,128)} %bitcast.18, f32[8,8,1024]{2,1,0:T(8,128)} %bitcast.15, f32[3,8,8,1024]{3,2,1,0:T(8,128)} %bitcast.13, s32[2,8,8,1024]{3,2,1,0:T(8,128)} %bitcast.14), custom_call_target="tpu_custom_call" | custom-call | flops 50000000 | bytes 20000000 | tf_op jit(solution)/shard_map/edge_terms/pallas_call | solution.py:197
  6.5 0.0 copy-start.5
  6.5 11.5 %all-to-all-start = ((f32[128,16,128]{2,1,0:T(8,128)}), f32[128,16,128]{2,1,0:T(8,128)S(1)}, u32[]{:S(2)}, u32[]{:S(2)}) async-start(f32[128,16,128]{2,1,0:T(8,128)} %bitcast.16), calls=%async_computation | async-start | bytes 2097152 | tf_op jit(solution)/shard_map/all_to_all | solution.py:594
  18.1 0.0 copy-done.5
  18.1 0.7 collective-permute-start
  18.7 0.0 collective-permute-done.sigma_ref
  18.7 18.8 %all-to-all-done = f32[128,16,128]{2,1,0:T(8,128)S(1)} async-done(((f32[128,16,128]{2,1,0:T(8,128)}), f32[128,16,128]{2,1,0:T(8,128)S(1)}, u32[]{:S(2)}, u32[]{:S(2)}) %all-to-all-start) | async-done | bytes 1048608 | tf_op jit(solution)/shard_map/all_to_all | solution.py:594
  37.5 1.8 %far_sums.1 = (f32[144,768]{1,0:T(8,128)S(1)}, f32[128,512]{1,0:T(8,128)S(1)}, s32[16,128]{1,0:T(8,128)S(1)}, f32[32,1024]{1,0:T(8,128)S(1)}) custom-call(f32[2048,128]{1,0:T(8,128)S(1)} %bitcast.10, f32[4,32,256]{2,1,0:T(8,128)S(1)} %collective-permute-done.sigma_ref), custom_call_target="tpu_custom_call" | custom-call | flops 800000000 | bytes 5000000 | tf_op jit(solution)/shard_map/far_sums/pallas_call | solution.py:356
  39.3 1.0 %collective-permute-start.1 = (f32[144,768]{1,0:T(8,128)S(1)}, f32[144,768]{1,0:T(8,128)S(1)}, u32[]{:S(2)}, u32[]{:S(2)}) collective-permute-start(f32[144,768]{1,0:T(8,128)S(1)} %get-tuple-element.12.far_ref), channel_id=1, source_target_pairs={{0,97},{1,2},{2,1},{3,4},{4,3},{5,6},{6,5},{7,14},{14,7},{15,12},{... | collective-permute-start | bytes 1327112 | tf_op jit(solution)/shard_map/ppermute | solution.py:607
  40.3 1.1 %near_sums.1.near_ref = f32[144,768]{1,0:T(8,128)S(1)} custom-call(f32[2048,128]{1,0:T(8,128)S(1)} %bitcast.11, f32[128,512]{1,0:T(8,128)S(1)} %get-tuple-element.13.mid_ref, f32[32,1024]{1,0:T(8,128)S(1)} %get-tuple-element.14.sig_ref), custom_call_target="tpu_custom_call" | custom-call | flops 300000000 | bytes 4000000 | tf_op jit(solution)/shard_map/near_sums/pallas_call | solution.py:407
  41.4 2.2 %collective-permute-start.2 = (f32[144,768]{1,0:T(8,128)S(1)}, f32[144,768]{1,0:T(8,128)S(1)}, u32[]{:S(2)}, u32[]{:S(2)}) collective-permute-start(f32[144,768]{1,0:T(8,128)S(1)} %near_sums.1.near_ref), channel_id=1, source_target_pairs={{0,1},{1,0},{2,3},{3,2},{4,5},{5,4},{6,7},{7,6},{14,15},{15,14},{1... | collective-permute-start | bytes 1327112 | tf_op jit(solution)/shard_map/ppermute | solution.py:609
  43.7 3.7 %collective-permute-done.1.before_ref = f32[144,768]{1,0:T(8,128)S(1)} collective-permute-done((f32[144,768]{1,0:T(8,128)S(1)}, f32[144,768]{1,0:T(8,128)S(1)}, u32[]{:S(2)}, u32[]{:S(2)}) %collective-permute-start.1) | collective-permute-done | bytes 442400 | tf_op jit(solution)/shard_map/ppermute | solution.py:607
  47.4 0.0 collective-permute-done.2.after_ref
  47.4 2.6 %sweeps.1 = f32[2048,128]{1,0:T(8,128)S(1)} custom-call(f32[144,768]{1,0:T(8,128)S(1)} %get-tuple-element.12.far_ref, f32[144,768]{1,0:T(8,128)S(1)} %near_sums.1.near_ref, f32[128,512]{1,0:T(8,128)S(1)} %get-tuple-element.13.mid_ref, f32[144,768]{1,0:T(8,128)S(1)} %collective-permute-done.1.before_ref, f32[144,768]{1,0:T(8,128)S(1)} %collective-permute-done.2.after_ref, ...), custom_call_target="tpu_custom_call" | custom-call | tf_op jit(solution)/shard_map/sweeps/pallas_call | solution.py:506
  50.0 0.0 copy-start
  50.0 0.0 copy-start.1
  50.0 0.0 copy-start.2
  50.0 0.0 copy-start.3
  50.0 0.0 copy-start.4
  50.0 24.1 %all_to_all.10 = f32[128,16,128]{2,1,0:T(8,128)S(1)} all-to-all(f32[128,16,128]{2,1,0:T(8,128)S(1)} %bitcast.9), channel_id=1, replica_groups=mesh['edge'=16,'node'=8] {'edge','node'}, dimensions={0} | all-to-all | bytes 2097152 | tf_op jit(solution)/shard_map/all_to_all | solution.py:594
  74.2 0.0 copy-done
  74.2 0.0 copy-done.1
  74.2 0.0 copy-done.2
  74.2 0.0 copy-done.3
  74.2 0.0 copy-done.4
  74.2 2.7 %lift.1 = f32[64,1024]{1,0:T(8,128)} custom-call(f32[2048,128]{1,0:T(8,128)S(1)} %bitcast.12, s32[1,1024]{1,0:T(1,128)S(1)} %copy-done.4, f32[64,1024]{1,0:T(8,128)S(1)} %copy-done.2, f32[3,64,1024]{2,1,0:T(8,128)S(1)} %copy-done, f32[64,1024]{1,0:T(8,128)S(1)} %copy-done.3, s32[2,64,1024]{2,1,0:T(8,128)S(1)} %copy-done.1), custom_call_target="tpu_custom_call" | custom-call | tf_op jit(solution)/shard_map/lift/pallas_call | solution.py:576
Async XLA Ops:
  6.5 11.5 %copy-start.5 = (f32[4,32,256]{2,1,0:T(8,128)S(1)}, f32[4,32,256]{2,1,0:T(8,128)}, u32[]{:S(2)}) copy-start(f32[4,32,256]{2,1,0:T(8,128)} %param.13) | copy-start | bytes 393220
  6.5 31.0 %all-to-all-start = ((f32[128,16,128]{2,1,0:T(8,128)}), f32[128,16,128]{2,1,0:T(8,128)S(1)}, u32[]{:S(2)}, u32[]{:S(2)}) async-start(f32[128,16,128]{2,1,0:T(8,128)} %bitcast.16), calls=%async_computation | async-start | bytes 2097152 | tf_op jit(solution)/shard_map/all_to_all | solution.py:594
  18.1 0.7 collective-permute-start
  39.3 8.1 %collective-permute-start.1 = (f32[144,768]{1,0:T(8,128)S(1)}, f32[144,768]{1,0:T(8,128)S(1)}, u32[]{:S(2)}, u32[]{:S(2)}) collective-permute-start(f32[144,768]{1,0:T(8,128)S(1)} %get-tuple-element.12.far_ref), channel_id=1, source_target_pairs={{0,97},{1,2},{2,1},{3,4},{4,3},{5,6},{6,5},{7,14},{14,7},{15,12},{... | collective-permute-start | bytes 1327112 | tf_op jit(solution)/shard_map/ppermute | solution.py:607
  41.4 6.0 %collective-permute-start.2 = (f32[144,768]{1,0:T(8,128)S(1)}, f32[144,768]{1,0:T(8,128)S(1)}, u32[]{:S(2)}, u32[]{:S(2)}) collective-permute-start(f32[144,768]{1,0:T(8,128)S(1)} %near_sums.1.near_ref), channel_id=1, source_target_pairs={{0,1},{1,0},{2,3},{3,2},{4,5},{5,4},{6,7},{7,6},{14,15},{15,14},{1... | collective-permute-start | bytes 1327112 | tf_op jit(solution)/shard_map/ppermute | solution.py:609
  50.0 24.2 %copy-start = (f32[3,64,1024]{2,1,0:T(8,128)S(1)}, f32[3,64,1024]{2,1,0:T(8,128)}, u32[]{:S(2)}) copy-start(f32[3,64,1024]{2,1,0:T(8,128)} %tan_ref.1) | copy-start | bytes 2359300
  50.0 24.2 %copy-start.1 = (s32[2,64,1024]{2,1,0:T(8,128)S(1)}, s32[2,64,1024]{2,1,0:T(8,128)}, u32[]{:S(2)}) copy-start(s32[2,64,1024]{2,1,0:T(8,128)} %ends_ref.1) | copy-start | bytes 1572868
  50.0 24.2 %copy-start.2 = (f32[64,1024]{1,0:T(8,128)S(1)}, f32[64,1024]{1,0:T(8,128)}, u32[]{:S(2)}) copy-start(f32[64,1024]{1,0:T(8,128)} %res_ref.1) | copy-start | bytes 786436
  50.0 24.2 %copy-start.3 = (f32[64,1024]{1,0:T(8,128)S(1)}, f32[64,1024]{1,0:T(8,128)}, u32[]{:S(2)}) copy-start(f32[64,1024]{1,0:T(8,128)} %jac_ref.1) | copy-start | bytes 786436
  50.0 24.2 %copy-start.4 = (s32[1,1024]{1,0:T(1,128)S(1)}, s32[1,1024]{1,0:T(1,128)}, u32[]{:S(2)}) copy-start(s32[1,1024]{1,0:T(1,128)} %get-tuple-element.16.slot_ref) | copy-start | bytes 12292

commit v6 on v5

--- a/solution.py
+++ b/solution.py
@@ -491,7 +491,7 @@
                 sol_scr[rows(tile), spot(s, half)] = value
         return 0
 
-    lax.fori_loop(0, 4, channel_step, 0)
+    lax.fori_loop(0, 4, channel_step, 0, unroll=2)
     for group in range(BLOCKS // 128):
         part = slice(group * 128, (group + 1) * 128)
         row_scr[part, :] = sol_scr[:, part].T

time: 77.1 us -> 77 us (level)
  no operation moved by 1% of the time
where the time goes in v6:
time: 77 us; the launch traced here: 76.8 us
  blocking collectives  24.1 us (31%)
  waiting for transfers between devices  22.5 us (29%)
  starting transfers between devices  15.4 us (20%)
  Pallas kernels  14.5 us (19%)
    all_to_all x1, blocking collectives, exchange(): lax.all_to_all(parts, RING, split_axis=0, concat_axis=0, tiled=True)  24.1 us
    all_to_all x1, waiting for transfers between devices, exchange(): lax.all_to_all(parts, RING, split_axis=0, concat_axis=0, tiled=True)  18.8 us
    all_to_all x1, starting transfers between devices, exchange(): lax.all_to_all(parts, RING, split_axis=0, concat_axis=0, tiled=True)  11.5 us
    pallas_call x1, Pallas kernels, edge_terms(): pl.pallas_call(terms_kernel, out_shape=(jax.ShapeDtypeStruct((SLOTS, ROW)...  6.52 us
    ppermute x1, waiting for transfers between devices, per_device(): before = lax.ppermute(far, RING, between)  3.75 us
    pallas_call x1, Pallas kernels, lift(): pl.pallas_call(lift_kernel, out_shape=jax.ShapeDtypeStruct((EDGES, BLOCKS...  2.7 us
    pallas_call x1, Pallas kernels, sweeps(): pl.pallas_call(sweeps_kernel, out_shape=jax.ShapeDtypeStruct((SLOTS, ROW)...  2.43 us
    ppermute x1, starting transfers between devices, per_device(): after = lax.ppermute(near, RING, within)  2.24 us
  transfers between devices with their start and end apart: 4, of which 2 were waited for; matrix products, arithmetic and copies ran while one was open for 0% of the time, Pallas kernels for 1%

profile of v6, /device:TPU:1, one launch (start us, length us, event | category | flops | bytes accessed | tf_op | source)
XLA Modules:
  0.0 76.8 jit_solution(13052423898367058415)
XLA Ops:
  0.0 6.5 %edge_terms.1 = (f32[2048,128]{1,0:T(8,128)}, s32[1,1024]{1,0:T(1,128)}) custom-call(s32[1,1024]{1,0:T(1,128)} %bitcast.17, s32[1,1024]{1,0:T(1,128)} %bitcast.18, f32[8,8,1024]{2,1,0:T(8,128)} %bitcast.15, f32[3,8,8,1024]{3,2,1,0:T(8,128)} %bitcast.13, s32[2,8,8,1024]{3,2,1,0:T(8,128)} %bitcast.14), custom_call_target="tpu_custom_call" | custom-call | flops 50000000 | bytes 20000000 | tf_op jit(solution)/shard_map/edge_terms/pallas_call | solution.py:197
  6.5 0.0 copy-start.5
  6.5 11.5 %all-to-all-start = ((f32[128,16,128]{2,1,0:T(8,128)}), f32[128,16,128]{2,1,0:T(8,128)S(1)}, u32[]{:S(2)}, u32[]{:S(2)}) async-start(f32[128,16,128]{2,1,0:T(8,128)} %bitcast.16), calls=%async_computation | async-start | bytes 2097152 | tf_op jit(solution)/shard_map/all_to_all | solution.py:594
  18.1 0.0 copy-done.5
  18.1 0.7 collective-permute-start
  18.7 0.0 collective-permute-done.sigma_ref
  18.7 18.8 %all-to-all-done = f32[128,16,128]{2,1,0:T(8,128)S(1)} async-done(((f32[128,16,128]{2,1,0:T(8,128)}), f32[128,16,128]{2,1,0:T(8,128)S(1)}, u32[]{:S(2)}, u32[]{:S(2)}) %all-to-all-start) | async-done | bytes 1048608 | tf_op jit(solution)/shard_map/all_to_all | solution.py:594
  37.5 1.8 %far_sums.1 = (f32[144,768]{1,0:T(8,128)S(1)}, f32[128,512]{1,0:T(8,128)S(1)}, s32[16,128]{1,0:T(8,128)S(1)}, f32[32,1024]{1,0:T(8,128)S(1)}) custom-call(f32[2048,128]{1,0:T(8,128)S(1)} %bitcast.10, f32[4,32,256]{2,1,0:T(8,128)S(1)} %collective-permute-done.sigma_ref), custom_call_target="tpu_custom_call" | custom-call | flops 800000000 | bytes 5000000 | tf_op jit(solution)/shard_map/far_sums/pallas_call | solution.py:356
  39.3 1.0 %collective-permute-start.1 = (f32[144,768]{1,0:T(8,128)S(1)}, f32[144,768]{1,0:T(8,128)S(1)}, u32[]{:S(2)}, u32[]{:S(2)}) collective-permute-start(f32[144,768]{1,0:T(8,128)S(1)} %get-tuple-element.12.far_ref), channel_id=1, source_target_pairs={{0,97},{1,2},{2,1},{3,4},{4,3},{5,6},{6,5},{7,14},{14,7},{15,12},{... | collective-permute-start | bytes 1327112 | tf_op jit(solution)/shard_map/ppermute | solution.py:607
  40.3 1.1 %near_sums.1.near_ref = f32[144,768]{1,0:T(8,128)S(1)} custom-call(f32[2048,128]{1,0:T(8,128)S(1)} %bitcast.11, f32[128,512]{1,0:T(8,128)S(1)} %get-tuple-element.13.mid_ref, f32[32,1024]{1,0:T(8,128)S(1)} %get-tuple-element.14.sig_ref), custom_call_target="tpu_custom_call" | custom-call | flops 300000000 | bytes 4000000 | tf_op jit(solution)/shard_map/near_sums/pallas_call | solution.py:407
  41.4 2.2 %collective-permute-start.2 = (f32[144,768]{1,0:T(8,128)S(1)}, f32[144,768]{1,0:T(8,128)S(1)}, u32[]{:S(2)}, u32[]{:S(2)}) collective-permute-start(f32[144,768]{1,0:T(8,128)S(1)} %near_sums.1.near_ref), channel_id=1, source_target_pairs={{0,1},{1,0},{2,3},{3,2},{4,5},{5,4},{6,7},{7,6},{14,15},{15,14},{1... | collective-permute-start | bytes 1327112 | tf_op jit(solution)/shard_map/ppermute | solution.py:609
  43.7 3.7 %collective-permute-done.1.before_ref = f32[144,768]{1,0:T(8,128)S(1)} collective-permute-done((f32[144,768]{1,0:T(8,128)S(1)}, f32[144,768]{1,0:T(8,128)S(1)}, u32[]{:S(2)}, u32[]{:S(2)}) %collective-permute-start.1) | collective-permute-done | bytes 442400 | tf_op jit(solution)/shard_map/ppermute | solution.py:607
  47.4 0.0 collective-permute-done.2.after_ref
  47.4 2.4 %sweeps.1 = f32[2048,128]{1,0:T(8,128)S(1)} custom-call(f32[144,768]{1,0:T(8,128)S(1)} %get-tuple-element.12.far_ref, f32[144,768]{1,0:T(8,128)S(1)} %near_sums.1.near_ref, f32[128,512]{1,0:T(8,128)S(1)} %get-tuple-element.13.mid_ref, f32[144,768]{1,0:T(8,128)S(1)} %collective-permute-done.1.before_ref, f32[144,768]{1,0:T(8,128)S(1)} %collective-permute-done.2.after_ref, ...), custom_call_target="tpu_custom_call" | custom-call | tf_op jit(solution)/shard_map/sweeps/pallas_call | solution.py:506
  49.8 0.0 copy-start
  49.9 0.0 copy-start.1
  49.9 0.0 copy-start.2
  49.9 0.0 copy-start.3
  49.9 0.0 copy-start.4
  49.9 24.1 %all_to_all.10 = f32[128,16,128]{2,1,0:T(8,128)S(1)} all-to-all(f32[128,16,128]{2,1,0:T(8,128)S(1)} %bitcast.9), channel_id=1, replica_groups=mesh['edge'=16,'node'=8] {'edge','node'}, dimensions={0} | all-to-all | bytes 2097152 | tf_op jit(solution)/shard_map/all_to_all | solution.py:594
  74.0 0.0 copy-done
  74.0 0.0 copy-done.1
  74.0 0.0 copy-done.2
  74.0 0.0 copy-done.3
  74.1 0.0 copy-done.4
  74.1 2.7 %lift.1 = f32[64,1024]{1,0:T(8,128)} custom-call(f32[2048,128]{1,0:T(8,128)S(1)} %bitcast.12, s32[1,1024]{1,0:T(1,128)S(1)} %copy-done.4, f32[64,1024]{1,0:T(8,128)S(1)} %copy-done.2, f32[3,64,1024]{2,1,0:T(8,128)S(1)} %copy-done, f32[64,1024]{1,0:T(8,128)S(1)} %copy-done.3, s32[2,64,1024]{2,1,0:T(8,128)S(1)} %copy-done.1), custom_call_target="tpu_custom_call" | custom-call | tf_op jit(solution)/shard_map/lift/pallas_call | solution.py:576
Async XLA Ops:
  6.5 11.5 %copy-start.5 = (f32[4,32,256]{2,1,0:T(8,128)S(1)}, f32[4,32,256]{2,1,0:T(8,128)}, u32[]{:S(2)}) copy-start(f32[4,32,256]{2,1,0:T(8,128)} %param.13) | copy-start | bytes 393220
  6.5 31.0 %all-to-all-start = ((f32[128,16,128]{2,1,0:T(8,128)}), f32[128,16,128]{2,1,0:T(8,128)S(1)}, u32[]{:S(2)}, u32[]{:S(2)}) async-start(f32[128,16,128]{2,1,0:T(8,128)} %bitcast.16), calls=%async_computation | async-start | bytes 2097152 | tf_op jit(solution)/shard_map/all_to_all | solution.py:594
  18.1 0.7 collective-permute-start
  39.3 8.1 %collective-permute-start.1 = (f32[144,768]{1,0:T(8,128)S(1)}, f32[144,768]{1,0:T(8,128)S(1)}, u32[]{:S(2)}, u32[]{:S(2)}) collective-permute-start(f32[144,768]{1,0:T(8,128)S(1)} %get-tuple-element.12.far_ref), channel_id=1, source_target_pairs={{0,97},{1,2},{2,1},{3,4},{4,3},{5,6},{6,5},{7,14},{14,7},{15,12},{... | collective-permute-start | bytes 1327112 | tf_op jit(solution)/shard_map/ppermute | solution.py:607
  41.4 6.0 %collective-permute-start.2 = (f32[144,768]{1,0:T(8,128)S(1)}, f32[144,768]{1,0:T(8,128)S(1)}, u32[]{:S(2)}, u32[]{:S(2)}) collective-permute-start(f32[144,768]{1,0:T(8,128)S(1)} %near_sums.1.near_ref), channel_id=1, source_target_pairs={{0,1},{1,0},{2,3},{3,2},{4,5},{5,4},{6,7},{7,6},{14,15},{15,14},{1... | collective-permute-start | bytes 1327112 | tf_op jit(solution)/shard_map/ppermute | solution.py:609
  49.8 24.2 %copy-start = (f32[3,64,1024]{2,1,0:T(8,128)S(1)}, f32[3,64,1024]{2,1,0:T(8,128)}, u32[]{:S(2)}) copy-start(f32[3,64,1024]{2,1,0:T(8,128)} %tan_ref.1) | copy-start | bytes 2359300
  49.9 24.2 %copy-start.1 = (s32[2,64,1024]{2,1,0:T(8,128)S(1)}, s32[2,64,1024]{2,1,0:T(8,128)}, u32[]{:S(2)}) copy-start(s32[2,64,1024]{2,1,0:T(8,128)} %ends_ref.1) | copy-start | bytes 1572868
  49.9 24.2 %copy-start.2 = (f32[64,1024]{1,0:T(8,128)S(1)}, f32[64,1024]{1,0:T(8,128)}, u32[]{:S(2)}) copy-start(f32[64,1024]{1,0:T(8,128)} %res_ref.1) | copy-start | bytes 786436
  49.9 24.2 %copy-start.3 = (f32[64,1024]{1,0:T(8,128)S(1)}, f32[64,1024]{1,0:T(8,128)}, u32[]{:S(2)}) copy-start(f32[64,1024]{1,0:T(8,128)} %jac_ref.1) | copy-start | bytes 786436
  49.9 24.2 %copy-start.4 = (s32[1,1024]{1,0:T(1,128)S(1)}, s32[1,1024]{1,0:T(1,128)}, u32[]{:S(2)}) copy-start(s32[1,1024]{1,0:T(1,128)} %get-tuple-element.16.slot_ref) | copy-start | bytes 12292
